TPU v7x, 128 devices: a whole 4x4x4 slice. The times are simulated.
128 devices in a mesh: row: 8 (over z, core), leaf: 16 (over y, x).
Axes of the slice: x: 4, y: 4, z: 4, core: 2. Of those that a mesh axis runs over, the one named last changes fastest.
Arguments:
- leaf_update: float32 [16384, 256], P(('leaf', 'row')), may hold values from -6 to 6
- rhs: float32 [3, 16384, 256], P(None, ('leaf', 'row')), may hold values from -6 to 6
- inv_top: bfloat16 [2, 16384, 16, 8, 128], P(None, 'leaf', None, 'row'), may hold values from -0.03125 to 0.03125
- inv_mid: bfloat16 [2, 16384, 8, 8, 128], P(None, 'leaf', None, 'row'), may hold values from -0.046875 to 0.046875
- inv_low: bfloat16 [2, 16384, 4, 8, 128], P(None, 'leaf', None, 'row'), may hold values from -0.0625 to 0.0625
- couple_mid: bfloat16 [2, 16384, 8, 8, 128], P(None, 'leaf', None, 'row'), may hold values from -0.046875 to 0.046875
- couple_low: bfloat16 [2, 16384, 4, 8, 128], P(None, 'leaf', None, 'row'), may hold values from -0.0625 to 0.0625
- block_map: int32 [3, 128], P(None, ('leaf', 'row')), may hold values from 0 to 127, as said below
Outputs:
- solution: float32 [3, 16384, 256], P(None, ('leaf', 'row'))
- leaf_solution: float32 [16384, 256], P(('leaf', 'row'))
Inputs may be any that keep to these rules, and one draw needn't show every extreme that they name: Device d of the group of a front holds rows d * 128 to (d + 1) * 128 - 1 of the front's separator part and the same rows of its update part, with d = p * 8 + r for group position p (leaf index modulo the group size) and row index r. block_map[k] is one to one within each parent, and a block held at row index r and group position p of a child lands on a parent block held at row index r and group position p or p + (group size of the parent) / 2. At level 0 every parent block receives one block.
All inputs are finite; a program needn't handle non-finite values.
Results may differ from a plain program's by a relative error of at most 0.012.
Values may be sent and summed in bfloat16 or wider, within the bound.
No kernel may reach another device: no remote copies, remote signals or barrier semaphores. Data moves between devices by JAX's collectives and lax.ppermute only.
A program may use at most 128 MiB of HBM per device.

v0:
```python
import jax
import jax.numpy as jnp
from jax import lax
from jax.sharding import PartitionSpec as P

BLOCK = 128


def partner_2(block, axis, distance):
    count = lax.axis_size(axis)
    route = []
    for low in range(count):
        high = low | 1 << distance
        if high != low and high < count:
            route += [(low, high), (high, low)]
    return lax.ppermute(block, axis, route)


def cut_along(value, dim, peers):
    lengths = value.shape
    blocks = value.reshape(*lengths[:dim], peers, lengths[dim] // peers, *lengths[dim + 1 :])
    return jnp.moveaxis(blocks, dim, 0)


def summed_on_arrival(value, axis, dim):
    peers = lax.axis_size(axis)
    blocks = lax.all_to_all(cut_along(value, dim, peers), axis, 0, 0, tiled=True)
    return jnp.sum(blocks, axis=0)


def laid_out(blocks, dim):
    lengths = list(blocks.shape[1:])
    lengths[dim] *= blocks.shape[0]
    return jnp.moveaxis(blocks, 0, dim).reshape(lengths)


def copy_for_each(value, axis):
    copies = jnp.broadcast_to(value, (lax.axis_size(axis), *value.shape))
    return lax.all_to_all(copies, axis, split_axis=0, concat_axis=0, tiled=True)


def collect(value, axis, dim):
    return laid_out(copy_for_each(value, axis), dim)


def complex_apply(real_part, imag_part, right_side, transpose):
    half_cols = right_side.shape[1] // 2
    if transpose:
        dim_numbers = (((0,), (0,)), ((), ()))
    else:
        dim_numbers = (((1,), (0,)), ((), ()))
    product_real = lax.dot_general(
        real_part, right_side, dim_numbers, preferred_element_type=jnp.float32
    )
    product_imag = lax.dot_general(
        imag_part, right_side, dim_numbers, preferred_element_type=jnp.float32
    )
    return jnp.concatenate(
        [
            product_real[:, :half_cols] - product_imag[:, half_cols:],
            product_real[:, half_cols:] + product_imag[:, :half_cols],
        ],
        axis=1,
    )


def panel_parts(panel_tile):
    merged = panel_tile.reshape(
        2, panel_tile.shape[1], panel_tile.shape[2] * panel_tile.shape[3] * panel_tile.shape[4]
    )
    return (merged[0], merged[1])


def subgroup_gather(vector, bit_count, leaf_pos):
    gathered = vector
    for bit_pos in range(bit_count):
        partner = partner_2(gathered, "leaf", bit_pos)
        upper_half = leaf_pos >> bit_pos & 1 == 1
        gathered = jnp.where(
            upper_half,
            jnp.concatenate([partner, gathered], axis=0),
            jnp.concatenate([gathered, partner], axis=0),
        )
    return gathered


def subgroup_sum(partial_value, bit_count, leaf_pos):
    total_sum = partial_value
    for bit_pos in reversed(range(bit_count)):
        half_rows = total_sum.shape[0] // 2
        upper_half = leaf_pos >> bit_pos & 1 == 1
        kept_half = jnp.where(upper_half, total_sum[half_rows:], total_sum[:half_rows])
        sent_half = jnp.where(upper_half, total_sum[:half_rows], total_sum[half_rows:])
        total_sum = kept_half + partner_2(sent_half, "leaf", bit_pos)
    return total_sum


def row_reduced(panel_tile, gathered):
    real_part, imag_part = panel_parts(panel_tile)
    return summed_on_arrival(complex_apply(real_part, imag_part, gathered, False), "row", 0)


def row_folded(panel_tile, vector_half):
    real_part, imag_part = panel_parts(panel_tile)
    return complex_apply(real_part, imag_part, collect(vector_half, "row", 0), True)


def slot_ids(position, row_pos, row_size, blocks_dev, sep_blocks, has_update):
    own_slots = (position * row_size + row_pos) * blocks_dev + jnp.arange(
        blocks_dev, dtype=jnp.int32
    )
    if has_update:
        return jnp.concatenate([own_slots, own_slots + sep_blocks])
    return own_slots


def extend_add(child_rows, targets, rhs_part, bit_count, has_update, leaf_pos, row_pos, row_size):
    bit_pos = bit_count - 1
    partner_rows, partner_targets = partner_2((child_rows, targets), "leaf", bit_pos)
    blocks_dev = targets.shape[0]
    group_size = 1 << bit_count
    position = leaf_pos & group_size - 1
    sep_blocks = group_size * row_size * blocks_dev
    slot_list = slot_ids(position, row_pos, row_size, blocks_dev, sep_blocks, has_update)
    candidates = jnp.concatenate([targets, partner_targets])
    columns = child_rows.shape[1]
    block_pool = jnp.concatenate([child_rows, partner_rows], axis=0).reshape(2 * blocks_dev, -1)
    selector = (slot_list[:, None] == candidates[None, :]).astype(jnp.float32)
    placed = jnp.dot(
        selector, block_pool, precision=lax.Precision.HIGHEST, preferred_element_type=jnp.float32
    ).reshape(-1, columns)
    slice_rows = rhs_part.shape[0]
    return (placed[:slice_rows] + rhs_part, placed[slice_rows:])


def extend_down(front_rows, targets, bit_count, leaf_pos, row_pos, row_size):
    bit_pos = bit_count - 1
    partner_rows = partner_2(front_rows, "leaf", bit_pos)
    blocks_dev = targets.shape[0]
    has_update = front_rows.shape[0] > blocks_dev * BLOCK
    group_size = 1 << bit_count
    position = leaf_pos & group_size - 1
    sep_blocks = group_size * row_size * blocks_dev
    own_slots = slot_ids(position, row_pos, row_size, blocks_dev, sep_blocks, has_update)
    partner_slots = slot_ids(
        position ^ group_size // 2, row_pos, row_size, blocks_dev, sep_blocks, has_update
    )
    columns = front_rows.shape[1]
    block_pool = jnp.concatenate([front_rows, partner_rows], axis=0).reshape(-1, BLOCK * columns)
    selector = (targets[:, None] == jnp.concatenate([own_slots, partner_slots])[None, :]).astype(
        jnp.float32
    )
    return jnp.dot(
        selector, block_pool, precision=lax.Precision.HIGHEST, preferred_element_type=jnp.float32
    ).reshape(-1, columns)


def shards(leaf_update, rhs, inv_top, inv_mid, inv_low, couple_mid, couple_low, block_map):
    leaf_pos = lax.axis_index("leaf")
    row_pos = lax.axis_index("row")
    row_size = lax.axis_size("row")
    leaf_bits = lax.axis_size("leaf").bit_length() - 1
    inverses = (inv_top, inv_mid, inv_low)
    couplings = (None, couple_mid, couple_low)
    children = leaf_update
    saved_y = [None, None, None]
    for level_index in (2, 1):
        bit_count = leaf_bits - level_index
        sep_part, update_part = extend_add(
            children,
            block_map[level_index],
            rhs[level_index],
            bit_count,
            True,
            leaf_pos,
            row_pos,
            row_size,
        )
        gathered = subgroup_gather(sep_part.astype(jnp.bfloat16), bit_count, leaf_pos)
        solved = row_reduced(inverses[level_index], gathered)
        saved_y[level_index] = solved
        gathered_y = subgroup_gather(solved.astype(jnp.bfloat16), bit_count, leaf_pos)
        children = update_part - row_reduced(couplings[level_index], gathered_y)
    sep_top, unused_rows = extend_add(
        children, block_map[0], rhs[0], leaf_bits, False, leaf_pos, row_pos, row_size
    )
    gathered = collect(sep_top.astype(jnp.bfloat16), "leaf", 0)
    y_top = row_reduced(inv_top, gathered)
    partial_value = row_folded(inv_top, y_top.astype(jnp.bfloat16))
    x_top = summed_on_arrival(partial_value, "leaf", 0)
    solutions = [x_top]
    front_rows = x_top
    for level_index in (1, 2):
        bit_count = leaf_bits - level_index
        x_update = extend_down(
            front_rows, block_map[level_index - 1], bit_count + 1, leaf_pos, row_pos, row_size
        )
        coupled = subgroup_sum(
            row_folded(couplings[level_index], x_update.astype(jnp.bfloat16)), bit_count, leaf_pos
        )
        reduced = saved_y[level_index] - coupled
        x_sep = subgroup_sum(
            row_folded(inverses[level_index], reduced.astype(jnp.bfloat16)), bit_count, leaf_pos
        )
        solutions.append(x_sep)
        front_rows = jnp.concatenate([x_sep, x_update], axis=0)
    leaf_solution = extend_down(
        front_rows, block_map[2], leaf_bits - 2, leaf_pos, row_pos, row_size
    )
    return (jnp.stack(solutions), leaf_solution)


def solution(mesh):
    return jax.shard_map(
        shards,
        mesh=mesh,
        in_specs=(
            P(("leaf", "row"), None),
            P(None, ("leaf", "row"), None),
            P(None, "leaf", None, "row", None),
            P(None, "leaf", None, "row", None),
            P(None, "leaf", None, "row", None),
            P(None, "leaf", None, "row", None),
            P(None, "leaf", None, "row", None),
            P(None, ("leaf", "row")),
        ),
        out_specs=(P(None, ("leaf", "row"), None), P(("leaf", "row"), None)),
        check_vma=False,
    )
```

profile of v0, /device:TPU:0, one launch (start us, length us, event | category | flops | bytes accessed | tf_op | source)
XLA Modules:
  0.0 445.0 jit_solution(5594407588404760829)
XLA Ops:
  0.6 1.4 fusion.153
  2.1 3.1 collective-permute-start.2
  7.3 1.3 pad_add_fusion.3
  8.5 3.3 collective-permute-done.3
  15.1 3.8 collective-permute-done.4
  19.5 1.7 fusion.151
  21.2 4.4 collective-permute-done.5
  25.6 1.8 convolution_bitcast_fusion.3
  27.4 1.5 convolution_bitcast_fusion.2
  29.2 21.3 %all_to_all.60 = f32[8,128,256]{1,2,0:T(8,128)S(1)} all-to-all(f32[8,128,256]{1,2,0:T(8,128)S(1)} %copy_bitcast_fusion.5), channel_id=1, replica_groups=mesh['row'=8,'leaf'=16] {'row'}, dimensions={0} | all-to-all | bytes 2097152 | tf_op jit(solution)/shard_map/all_to_all | solution.py:27
  51.2 3.8 collective-permute-done.6
  56.3 5.2 %collective-permute-done.7 = bf16[256,256]{0,1:T(8,128)(2,1)S(1)} collective-permute-done((bf16[256,256]{0,1:T(8,128)(2,1)S(1)}, bf16[256,256]{0,1:T(8,128)(2,1)S(1)}, u32[]{:S(2)}, u32[]{:S(2)}) %collective-permute-start.7) | collective-permute-done | bytes 131104 | tf_op jit(solution)/shard_map/ppermute | solution.py:16
  63.8 3.6 all-to-all-start.1
  67.4 1.7 collective-permute-start.1
  69.2 14.1 %all-to-all-done.1 = f32[8,128,256]{1,2,0:T(8,128)S(1)} async-done(((f32[8,128,256]{1,2,0:T(8,128)}), f32[8,128,256]{1,2,0:T(8,128)S(1)}, u32[]{:S(2)}, u32[]{:S(2)}) %all-to-all-start.1) | async-done | bytes 1048608 | tf_op jit(solution)/shard_map/all_to_all | solution.py:27
  83.3 1.7 collective-permute-start.8
  85.2 1.4 pad_add_fusion.1
  86.6 1.9 collective-permute-done.8
  90.9 3.8 collective-permute-done.9
  95.2 6.0 %collective-permute-done.10 = bf16[256,256]{0,1:T(8,128)(2,1)S(1)} collective-permute-done((bf16[256,256]{0,1:T(8,128)(2,1)S(1)}, bf16[256,256]{0,1:T(8,128)(2,1)S(1)}, u32[]{:S(2)}, u32[]{:S(2)}) %collective-permute-start.10) | collective-permute-done | bytes 131104 | tf_op jit(solution)/shard_map/ppermute | solution.py:16
  101.3 2.1 collective-permute-start.11
  103.5 2.5 fusion.149
  106.0 2.3 collective-permute-done.11
  110.0 18.5 %all_to_all.61 = f32[8,128,256]{1,2,0:T(8,128)S(1)} all-to-all(f32[8,128,256]{1,2,0:T(8,128)S(1)} %copy_bitcast_fusion.3), channel_id=1, replica_groups=mesh['row'=8,'leaf'=16] {'row'}, dimensions={0} | all-to-all | bytes 2097152 | tf_op jit(solution)/shard_map/all_to_all | solution.py:27
  129.2 3.8 collective-permute-done.12
  133.6 6.0 %collective-permute-done.13 = bf16[256,256]{0,1:T(8,128)(2,1)S(1)} collective-permute-done((bf16[256,256]{0,1:T(8,128)(2,1)S(1)}, bf16[256,256]{0,1:T(8,128)(2,1)S(1)}, u32[]{:S(2)}, u32[]{:S(2)}) %collective-permute-start.13) | collective-permute-done | bytes 131104 | tf_op jit(solution)/shard_map/ppermute | solution.py:16
  139.7 1.7 collective-permute-start.14
  141.4 2.5 fusion.148
  143.9 2.3 collective-permute-done.14
  148.9 3.6 all-to-all-start.3
  152.6 15.7 %all-to-all-done.3 = f32[8,128,256]{1,2,0:T(8,128)S(1)} async-done(((f32[8,128,256]{1,2,0:T(8,128)}), f32[8,128,256]{1,2,0:T(8,128)S(1)}, u32[]{:S(2)}, u32[]{:S(2)}) %all-to-all-start.3) | async-done | bytes 1048608 | tf_op jit(solution)/shard_map/all_to_all | solution.py:27
  168.4 3.3 collective-permute-start.15
  172.1 3.0 collective-permute-done.15
  175.4 1.4 collective-permute-done
  176.9 2.0 fusion.105
  180.9 3.7 all-to-all-start.4
  184.5 6.2 %fusion.147 = (bf16[1,1024,16,1,128]{4,2,3,1,0:T(8,128)(2,1)}, bf16[1,1024,16,1,128]{4,2,3,1,0:T(8,128)(2,1)}) fusion(bf16[2,1024,16,1,128]{4,2,3,1,0:T(8,128)(2,1)} %param.10), kind=kLoop, calls=%fused_computation.230 | loop fusion | bytes 16777216 | tf_op jit(solution)/shard_map/slice | solution.py:71
  190.8 10.1 %all-to-all-done.4 = bf16[16,128,256]{2,1,0:T(8,128)(2,1)S(1)} async-done(((bf16[16,128,256]{2,1,0:T(8,128)(2,1)}), bf16[16,128,256]{2,1,0:T(8,128)(2,1)S(1)}, u32[]{:S(2)}, u32[]{:S(2)}) %all-to-all-start.4) | async-done | bytes 1048608 | tf_op jit(solution)/shard_map/all_to_all | solution.py:39
  200.9 3.7 fusion.66
  204.5 1.3 fusion.69
  206.1 18.5 %all_to_all.62 = f32[8,128,256]{1,2,0:T(8,128)S(1)} all-to-all(f32[8,128,256]{1,2,0:T(8,128)S(1)} %copy_bitcast_fusion.1), channel_id=1, replica_groups=mesh['row'=8,'leaf'=16] {'row'}, dimensions={0} | all-to-all | bytes 2097152 | tf_op jit(solution)/shard_map/all_to_all | solution.py:27
  224.8 13.0 %all_to_all.63 = bf16[8,128,256]{2,1,0:T(8,128)(2,1)S(1)} all-to-all(bf16[8,128,256]{2,1,0:T(8,128)(2,1)S(1)} %broadcast_in_dim.13), channel_id=1, replica_groups=mesh['row'=8,'leaf'=16] {'row'}, dimensions={0} | all-to-all | bytes 1048576 | tf_op jit(solution)/shard_map/all_to_all | solution.py:39
  237.8 3.6 fusion.12
  241.4 1.3 fusion.15
  243.2 31.0 %all_to_all.64 = f32[16,128,256]{1,2,0:T(8,128)S(1)} all-to-all(f32[16,128,256]{1,2,0:T(8,128)S(1)} %copy_bitcast_fusion), channel_id=1, replica_groups=mesh['row'=8,'leaf'=16] {'leaf'}, dimensions={0} | all-to-all | bytes 4194304 | tf_op jit(solution)/shard_map/all_to_all | solution.py:27
  275.3 5.6 %collective-permute-done.16 = f32[128,256]{0,1:T(8,128)S(1)} collective-permute-done((f32[128,256]{0,1:T(8,128)S(1)}, f32[128,256]{0,1:T(8,128)S(1)}, u32[]{:S(2)}, u32[]{:S(2)}) %collective-permute-start.16) | collective-permute-done | bytes 131104 | tf_op jit(solution)/shard_map/ppermute | solution.py:16
  281.3 1.3 fusion.106
  282.8 12.8 %all_to_all.65 = bf16[8,128,256]{2,1,0:T(8,128)(2,1)S(1)} all-to-all(bf16[8,128,256]{2,1,0:T(8,128)(2,1)S(1)} %broadcast_in_dim.28), channel_id=1, replica_groups=mesh['row'=8,'leaf'=16] {'row'}, dimensions={0} | all-to-all | bytes 1048576 | tf_op jit(solution)/shard_map/all_to_all | solution.py:39
  298.3 13.3 %collective-permute-done.17 = f32[512,256]{0,1:T(8,128)S(1)} collective-permute-done((f32[512,256]{0,1:T(8,128)S(1)}, f32[512,256]{0,1:T(8,128)S(1)}, u32[]{:S(2)}, u32[]{:S(2)}) %collective-permute-start.17) | collective-permute-done | bytes 524320 | tf_op jit(solution)/shard_map/ppermute | solution.py:16
  312.7 7.5 %collective-permute-done.18 = f32[256,256]{0,1:T(8,128)S(1)} collective-permute-done((f32[256,256]{0,1:T(8,128)S(1)}, f32[256,256]{0,1:T(8,128)S(1)}, u32[]{:S(2)}, u32[]{:S(2)}) %collective-permute-start.18) | collective-permute-done | bytes 262176 | tf_op jit(solution)/shard_map/ppermute | solution.py:16
  320.9 4.4 collective-permute-done.19
  325.5 12.8 %all_to_all.66 = bf16[8,128,256]{2,1,0:T(8,128)(2,1)S(1)} all-to-all(bf16[8,128,256]{2,1,0:T(8,128)(2,1)S(1)} %broadcast_in_dim.29), channel_id=1, replica_groups=mesh['row'=8,'leaf'=16] {'row'}, dimensions={0} | all-to-all | bytes 1048576 | tf_op jit(solution)/shard_map/all_to_all | solution.py:39
  341.6 12.7 %collective-permute-done.20 = f32[512,256]{0,1:T(8,128)S(1)} collective-permute-done((f32[512,256]{0,1:T(8,128)S(1)}, f32[512,256]{0,1:T(8,128)S(1)}, u32[]{:S(2)}, u32[]{:S(2)}) %collective-permute-start.20) | collective-permute-done | bytes 524320 | tf_op jit(solution)/shard_map/ppermute | solution.py:16
  355.3 7.5 %collective-permute-done.21 = f32[256,256]{0,1:T(8,128)S(1)} collective-permute-done((f32[256,256]{0,1:T(8,128)S(1)}, f32[256,256]{0,1:T(8,128)S(1)}, u32[]{:S(2)}, u32[]{:S(2)}) %collective-permute-start.21) | collective-permute-done | bytes 262176 | tf_op jit(solution)/shard_map/ppermute | solution.py:16
  363.5 4.4 collective-permute-done.22
  368.6 5.8 %collective-permute-done.23 = f32[256,256]{0,1:T(8,128)S(1)} collective-permute-done((f32[256,256]{0,1:T(8,128)S(1)}, f32[256,256]{0,1:T(8,128)S(1)}, u32[]{:S(2)}, u32[]{:S(2)}) %collective-permute-start.23) | collective-permute-done | bytes 262176 | tf_op jit(solution)/shard_map/ppermute | solution.py:16
  375.0 1.3 fusion.97
  376.6 12.9 %all_to_all.67 = bf16[8,128,256]{2,1,0:T(8,128)(2,1)S(1)} all-to-all(bf16[8,128,256]{2,1,0:T(8,128)(2,1)S(1)} %broadcast_in_dim.30), channel_id=1, replica_groups=mesh['row'=8,'leaf'=16] {'row'}, dimensions={0} | all-to-all | bytes 1048576 | tf_op jit(solution)/shard_map/all_to_all | solution.py:39
  391.7 8.4 %collective-permute-done.24 = f32[256,256]{0,1:T(8,128)S(1)} collective-permute-done((f32[256,256]{0,1:T(8,128)S(1)}, f32[256,256]{0,1:T(8,128)S(1)}, u32[]{:S(2)}, u32[]{:S(2)}) %collective-permute-start.24) | collective-permute-done | bytes 262176 | tf_op jit(solution)/shard_map/ppermute | solution.py:16
  400.8 4.4 collective-permute-done.25
  405.4 12.9 %all_to_all.68 = bf16[8,128,256]{2,1,0:T(8,128)(2,1)S(1)} all-to-all(bf16[8,128,256]{2,1,0:T(8,128)(2,1)S(1)} %broadcast_in_dim.31), channel_id=1, replica_groups=mesh['row'=8,'leaf'=16] {'row'}, dimensions={0} | all-to-all | bytes 1048576 | tf_op jit(solution)/shard_map/all_to_all | solution.py:39
  420.3 8.4 %collective-permute-done.26 = f32[256,256]{0,1:T(8,128)S(1)} collective-permute-done((f32[256,256]{0,1:T(8,128)S(1)}, f32[256,256]{0,1:T(8,128)S(1)}, u32[]{:S(2)}, u32[]{:S(2)}) %collective-permute-start.26) | collective-permute-done | bytes 262176 | tf_op jit(solution)/shard_map/ppermute | solution.py:16
  429.5 4.9 %collective-permute-done.27 = f32[128,256]{0,1:T(8,128)S(1)} collective-permute-done((f32[128,256]{0,1:T(8,128)S(1)}, f32[128,256]{0,1:T(8,128)S(1)}, u32[]{:S(2)}, u32[]{:S(2)}) %collective-permute-start.27) | collective-permute-done | bytes 131104 | tf_op jit(solution)/shard_map/ppermute | solution.py:16
  435.7 6.7 %collective-permute-done.28 = f32[256,256]{0,1:T(8,128)S(1)} collective-permute-done((f32[256,256]{0,1:T(8,128)S(1)}, f32[256,256]{0,1:T(8,128)S(1)}, u32[]{:S(2)}, u32[]{:S(2)}) %collective-permute-start.28) | collective-permute-done | bytes 262176 | tf_op jit(solution)/shard_map/ppermute | solution.py:16
  (188 shorter events, 45.6 us)
Async XLA Ops:
  0.6 18.9 %copy-start.2 = (bf16[2,1024,4,1,128]{4,2,3,1,0:T(4,128)(2,1)S(1)}, bf16[2,1024,4,1,128]{4,2,3,1,0:T(4,128)(2,1)}, u32[]{:S(2)}) copy-start(bf16[2,1024,4,1,128]{4,2,3,1,0:T(4,128)(2,1)} %param.12) | copy-start | bytes 6291460
  2.1 5.2 %collective-permute-start.2 = (s32[1]{0:T(128)}, s32[1]{0:T(128)}, u32[]{:S(2)}, u32[]{:S(2)}) collective-permute-start(s32[1]{0:T(128)} %bitcast.5), channel_id=1, source_target_pairs={{0,2},{2,0},{1,3},{3,1},{4,6},{6,4},{5,7},{7,5},{8,10},{10,8},{9,1... | collective-permute-start | bytes 20 | tf_op jit(solution)/shard_map/ppermute | solution.py:16
  5.2 6.7 %collective-permute-start.3 = (f32[128,256]{1,0:T(8,128)}, f32[128,256]{1,0:T(8,128)S(1)}, u32[]{:S(2)}, u32[]{:S(2)}) collective-permute-start(f32[128,256]{1,0:T(8,128)} %param.8), channel_id=1, source_target_pairs={{0,2},{2,0},{1,3},{3,1},{4,6},{6,4},{5,7},{7,5},{8,10},{10,8},{9,1... | collective-permute-start | bytes 393224 | tf_op jit(solution)/shard_map/ppermute | solution.py:16
  14.4 4.4 collective-permute-start.4
  18.9 6.7 %collective-permute-start.5 = (bf16[256,256]{0,1:T(8,128)(2,1)S(1)}, bf16[256,256]{0,1:T(8,128)(2,1)}, u32[]{:S(2)}, u32[]{:S(2)}) collective-permute-start(bf16[256,256]{0,1:T(8,128)(2,1)S(1)} %maximum_select_fusion.6), channel_id=1, source_target_pairs={{0,2},{2,0},{1,3},{3,1},{4,6},{6,4},{5,7},{7,5},{8,10},{10,8},{9,1... | collective-permute-start | bytes 393224 | tf_op jit(solution)/shard_map/ppermute | solution.py:16
  21.2 7.7 %copy-start.12 = (bf16[1,1024,4,1,128]{4,2,3,1,0:T(4,128)(2,1)}, bf16[1,1024,4,1,128]{4,2,3,1,0:T(4,128)(2,1)S(1)}, u32[]{:S(2)}) copy-start(bf16[1,1024,4,1,128]{4,2,3,1,0:T(4,128)(2,1)S(1)} %get-tuple-element.39) | copy-start | bytes 3145732
  29.2 26.4 %copy-start.3 = (bf16[2,1024,4,1,128]{4,2,3,1,0:T(4,128)(2,1)S(1)}, bf16[2,1024,4,1,128]{4,2,3,1,0:T(4,128)(2,1)}, u32[]{:S(2)}) copy-start(bf16[2,1024,4,1,128]{4,2,3,1,0:T(4,128)(2,1)} %param.14) | copy-start | bytes 6291460
  50.6 4.3 collective-permute-start.6
  55.0 6.6 %collective-permute-start.7 = (bf16[256,256]{0,1:T(8,128)(2,1)S(1)}, bf16[256,256]{0,1:T(8,128)(2,1)S(1)}, u32[]{:S(2)}, u32[]{:S(2)}) collective-permute-start(bf16[256,256]{0,1:T(8,128)(2,1)S(1)} %maximum_select_fusion.7), channel_id=1, source_target_pairs={{0,2},{2,0},{1,3},{3,1},{4,6},{6,4},{5,7},{7,5},{8,10},{10,8},{9,1... | collective-permute-start | bytes 393224 | tf_op jit(solution)/shard_map/ppermute | solution.py:16
  56.3 6.2 %copy-start.15 = (bf16[1,1024,4,1,128]{4,2,3,1,0:T(4,128)(2,1)}, bf16[1,1024,4,1,128]{4,2,3,1,0:T(4,128)(2,1)S(1)}, u32[]{:S(2)}) copy-start(bf16[1,1024,4,1,128]{4,2,3,1,0:T(4,128)(2,1)S(1)} %get-tuple-element.35) | copy-start | bytes 3145732
  56.3 6.2 %copy-start.17 = (bf16[1,1024,4,1,128]{4,2,3,1,0:T(4,128)(2,1)}, bf16[1,1024,4,1,128]{4,2,3,1,0:T(4,128)(2,1)S(1)}, u32[]{:S(2)}) copy-start(bf16[1,1024,4,1,128]{4,2,3,1,0:T(4,128)(2,1)S(1)} %get-tuple-element.34) | copy-start | bytes 3145732
  63.8 19.4 %all-to-all-start.1 = ((f32[8,128,256]{1,2,0:T(8,128)}), f32[8,128,256]{1,2,0:T(8,128)S(1)}, u32[]{:S(2)}, u32[]{:S(2)}) async-start(f32[8,128,256]{1,2,0:T(8,128)} %copy_bitcast_fusion.4), calls=%async_computation.1 | async-start | bytes 2097152 | tf_op jit(solution)/shard_map/all_to_all | solution.py:27
  67.4 17.8 %collective-permute-start.1 = (s32[1]{0:T(128)}, s32[1]{0:T(128)}, u32[]{:S(2)}, u32[]{:S(2)}) collective-permute-start(s32[1]{0:T(128)} %bitcast.3), channel_id=1, source_target_pairs={{0,4},{4,0},{1,5},{5,1},{2,6},{6,2},{3,7},{7,3},{8,12},{12,8},{9,1... | collective-permute-start | bytes 20 | tf_op jit(solution)/shard_map/ppermute | solution.py:16
  83.3 5.1 %collective-permute-start.8 = (f32[128,256]{0,1:T(8,128)S(1)}, f32[128,256]{0,1:T(8,128)S(1)}, u32[]{:S(2)}, u32[]{:S(2)}) collective-permute-start(f32[128,256]{0,1:T(8,128)S(1)} %sub.44), channel_id=1, source_target_pairs={{0,4},{4,0},{1,5},{5,1},{2,6},{6,2},{3,7},{7,3},{8,12},{12,8},{9,1... | collective-permute-start | bytes 393224 | tf_op jit(solution)/shard_map/ppermute | solution.py:16
  90.3 4.3 collective-permute-start.9
  94.7 6.6 %collective-permute-start.10 = (bf16[256,256]{0,1:T(8,128)(2,1)S(1)}, bf16[256,256]{0,1:T(8,128)(2,1)S(1)}, u32[]{:S(2)}, u32[]{:S(2)}) collective-permute-start(bf16[256,256]{0,1:T(8,128)(2,1)S(1)} %maximum_select_fusion.8), channel_id=1, source_target_pairs={{0,2},{2,0},{1,3},{3,1},{4,6},{6,4},{5,7},{7,5},{8,10},{10,8},{9,1... | collective-permute-start | bytes 393224 | tf_op jit(solution)/shard_map/ppermute | solution.py:16
  101.3 6.9 %collective-permute-start.11 = (bf16[512,256]{0,1:T(8,128)(2,1)S(1)}, bf16[512,256]{0,1:T(8,128)(2,1)S(1)}, u32[]{:S(2)}, u32[]{:S(2)}) collective-permute-start(bf16[512,256]{0,1:T(8,128)(2,1)S(1)} %maximum_select_fusion.4), channel_id=1, source_target_pairs={{0,4},{4,0},{1,5},{5,1},{2,6},{6,2},{3,7},{7,3},{8,12},{12,8},{9,1... | collective-permute-start | bytes 786440 | tf_op jit(solution)/shard_map/ppermute | solution.py:16
  106.0 3.1 copy-start.6
  106.0 3.1 copy-start.4
  128.6 4.3 collective-permute-start.12
  133.0 6.6 %collective-permute-start.13 = (bf16[256,256]{0,1:T(8,128)(2,1)S(1)}, bf16[256,256]{0,1:T(8,128)(2,1)S(1)}, u32[]{:S(2)}, u32[]{:S(2)}) collective-permute-start(bf16[256,256]{0,1:T(8,128)(2,1)S(1)} %maximum_select_fusion.9), channel_id=1, source_target_pairs={{0,2},{2,0},{1,3},{3,1},{4,6},{6,4},{5,7},{7,5},{8,10},{10,8},{9,1... | collective-permute-start | bytes 393224 | tf_op jit(solution)/shard_map/ppermute | solution.py:16
  139.7 6.5 %collective-permute-start.14 = (bf16[512,256]{0,1:T(8,128)(2,1)S(1)}, bf16[512,256]{0,1:T(8,128)(2,1)S(1)}, u32[]{:S(2)}, u32[]{:S(2)}) collective-permute-start(bf16[512,256]{0,1:T(8,128)(2,1)S(1)} %maximum_select_fusion.5), channel_id=1, source_target_pairs={{0,4},{4,0},{1,5},{5,1},{2,6},{6,2},{3,7},{7,3},{8,12},{12,8},{9,1... | collective-permute-start | bytes 786440 | tf_op jit(solution)/shard_map/ppermute | solution.py:16
  143.8 3.1 copy-start.10
  143.9 3.1 copy-start.8
  148.9 19.4 %all-to-all-start.3 = ((f32[8,128,256]{1,2,0:T(8,128)}), f32[8,128,256]{1,2,0:T(8,128)S(1)}, u32[]{:S(2)}, u32[]{:S(2)}) async-start(f32[8,128,256]{1,2,0:T(8,128)} %copy_bitcast_fusion.2), calls=%async_computation.3 | async-start | bytes 2097152 | tf_op jit(solution)/shard_map/all_to_all | solution.py:27
  168.4 6.6 %collective-permute-start.15 = (f32[128,256]{0,1:T(8,128)S(1)}, f32[128,256]{0,1:T(8,128)S(1)}, u32[]{:S(2)}, u32[]{:S(2)}) collective-permute-start(f32[128,256]{0,1:T(8,128)S(1)} %sub.47), channel_id=1, source_target_pairs={{0,8},{8,0},{1,9},{9,1},{2,10},{10,2},{3,11},{11,3},{4,12},{12,4},... | collective-permute-start | bytes 393224 | tf_op jit(solution)/shard_map/ppermute | solution.py:16
  171.7 5.1 %collective-permute-start = (s32[1]{0:T(128)}, s32[1]{0:T(128)}, u32[]{:S(2)}, u32[]{:S(2)}) collective-permute-start(s32[1]{0:T(128)} %bitcast), channel_id=1, source_target_pairs={{0,8},{8,0},{1,9},{9,1},{2,10},{10,2},{3,11},{11,3},{4,12},{12,4},... | collective-permute-start | bytes 20 | tf_op jit(solution)/shard_map/ppermute | solution.py:16
  180.9 20.0 %all-to-all-start.4 = ((bf16[16,128,256]{2,1,0:T(8,128)(2,1)}), bf16[16,128,256]{2,1,0:T(8,128)(2,1)S(1)}, u32[]{:S(2)}, u32[]{:S(2)}) async-start(bf16[16,128,256]{2,1,0:T(8,128)(2,1)} %broadcast_in_dim.12), calls=%async_computation.4 | async-start | bytes 2097152 | tf_op jit(solution)/shard_map/all_to_all | solution.py:39
  200.9 3.7 copy-start
  237.8 3.6 copy-start.1
  274.4 6.6 %collective-permute-start.16 = (f32[128,256]{0,1:T(8,128)S(1)}, f32[128,256]{0,1:T(8,128)S(1)}, u32[]{:S(2)}, u32[]{:S(2)}) collective-permute-start(f32[128,256]{0,1:T(8,128)S(1)} %reduce_sum.59), channel_id=1, source_target_pairs={{0,8},{8,0},{1,9},{9,1},{2,10},{10,2},{3,11},{11,3},{4,12},{12,4},... | collective-permute-start | bytes 393224 | tf_op jit(solution)/shard_map/ppermute | solution.py:16
  275.3 20.3 %copy-start.11 = (bf16[1,1024,8,1,128]{4,2,3,1,0:T(8,128)(2,1)S(1)}, bf16[1,1024,8,1,128]{4,2,3,1,0:T(8,128)(2,1)}, u32[]{:S(2)}) copy-start(bf16[1,1024,8,1,128]{4,2,3,1,0:T(8,128)(2,1)} %copy-done.10) | copy-start | bytes 6291460
  295.6 1.6 copy-start.9
  298.2 13.4 %collective-permute-start.17 = (f32[512,256]{0,1:T(8,128)S(1)}, f32[512,256]{0,1:T(8,128)S(1)}, u32[]{:S(2)}, u32[]{:S(2)}) collective-permute-start(f32[512,256]{0,1:T(8,128)S(1)} %broadcast_select_fusion.1), channel_id=1, source_target_pairs={{0,4},{4,0},{1,5},{5,1},{2,6},{6,2},{3,7},{7,3},{8,12},{12,8},{9,1... | collective-permute-start | bytes 1572872 | tf_op jit(solution)/shard_map/ppermute | solution.py:16
  311.8 26.5 %copy-start.7 = (bf16[1,1024,8,1,128]{4,2,3,1,0:T(8,128)(2,1)S(1)}, bf16[1,1024,8,1,128]{4,2,3,1,0:T(8,128)(2,1)}, u32[]{:S(2)}) copy-start(bf16[1,1024,8,1,128]{4,2,3,1,0:T(8,128)(2,1)} %copy-done.6) | copy-start | bytes 6291460
  311.8 8.3 %collective-permute-start.18 = (f32[256,256]{0,1:T(8,128)S(1)}, f32[256,256]{0,1:T(8,128)S(1)}, u32[]{:S(2)}, u32[]{:S(2)}) collective-permute-start(f32[256,256]{0,1:T(8,128)S(1)} %slice_select_fusion.1), channel_id=1, source_target_pairs={{0,2},{2,0},{1,3},{3,1},{4,6},{6,4},{5,7},{7,5},{8,10},{10,8},{9,1... | collective-permute-start | bytes 786440 | tf_op jit(solution)/shard_map/ppermute | solution.py:16
  320.2 5.0 %collective-permute-start.19 = (f32[128,256]{0,1:T(8,128)S(1)}, f32[128,256]{0,1:T(8,128)S(1)}, u32[]{:S(2)}, u32[]{:S(2)}) collective-permute-start(f32[128,256]{0,1:T(8,128)S(1)} %slice_select_fusion.5), channel_id=1, source_target_pairs={{0,1},{1,0},{2,3},{3,2},{4,5},{5,4},{6,7},{7,6},{8,9},{9,8},{10,11... | collective-permute-start | bytes 393224 | tf_op jit(solution)/shard_map/ppermute | solution.py:16
  338.3 1.6 copy-start.5
  340.9 13.4 %collective-permute-start.20 = (f32[512,256]{0,1:T(8,128)S(1)}, f32[512,256]{0,1:T(8,128)S(1)}, u32[]{:S(2)}, u32[]{:S(2)}) collective-permute-start(f32[512,256]{0,1:T(8,128)S(1)} %broadcast_select_fusion), channel_id=1, source_target_pairs={{0,4},{4,0},{1,5},{5,1},{2,6},{6,2},{3,7},{7,3},{8,12},{12,8},{9,1... | collective-permute-start | bytes 1572872 | tf_op jit(solution)/shard_map/ppermute | solution.py:16
  354.4 8.3 %collective-permute-start.21 = (f32[256,256]{0,1:T(8,128)S(1)}, f32[256,256]{0,1:T(8,128)S(1)}, u32[]{:S(2)}, u32[]{:S(2)}) collective-permute-start(f32[256,256]{0,1:T(8,128)S(1)} %slice_select_fusion), channel_id=1, source_target_pairs={{0,2},{2,0},{1,3},{3,1},{4,6},{6,4},{5,7},{7,5},{8,10},{10,8},{9,1... | collective-permute-start | bytes 786440 | tf_op jit(solution)/shard_map/ppermute | solution.py:16
  362.9 5.0 %collective-permute-start.22 = (f32[128,256]{0,1:T(8,128)S(1)}, f32[128,256]{0,1:T(8,128)S(1)}, u32[]{:S(2)}, u32[]{:S(2)}) collective-permute-start(f32[128,256]{0,1:T(8,128)S(1)} %slice_select_fusion.4), channel_id=1, source_target_pairs={{0,1},{1,0},{2,3},{3,2},{4,5},{5,4},{6,7},{7,6},{8,9},{9,8},{10,11... | collective-permute-start | bytes 393224 | tf_op jit(solution)/shard_map/ppermute | solution.py:16
  368.0 6.5 %collective-permute-start.23 = (f32[256,256]{0,1:T(8,128)S(1)}, f32[256,256]{0,1:T(8,128)S(1)}, u32[]{:S(2)}, u32[]{:S(2)}) collective-permute-start(f32[256,256]{0,1:T(8,128)S(1)} %pad_maximum_fusion.11), channel_id=1, source_target_pairs={{0,4},{4,0},{1,5},{5,1},{2,6},{6,2},{3,7},{7,3},{8,12},{12,8},{9,1... | collective-permute-start | bytes 786440 | tf_op jit(solution)/shard_map/ppermute | solution.py:16
  374.7 14.8 %copy-start.18 = (bf16[1,1024,4,1,128]{4,2,3,1,0:T(4,128)(2,1)S(1)}, bf16[1,1024,4,1,128]{4,2,3,1,0:T(4,128)(2,1)}, u32[]{:S(2)}) copy-start(bf16[1,1024,4,1,128]{4,2,3,1,0:T(4,128)(2,1)} %copy-done.17) | copy-start | bytes 3145732
  376.4 13.6 %copy-start.16 = (bf16[1,1024,4,1,128]{4,2,3,1,0:T(4,128)(2,1)S(1)}, bf16[1,1024,4,1,128]{4,2,3,1,0:T(4,128)(2,1)}, u32[]{:S(2)}) copy-start(bf16[1,1024,4,1,128]{4,2,3,1,0:T(4,128)(2,1)} %copy-done.15) | copy-start | bytes 3145732
  390.6 27.8 %copy-start.14 = (bf16[1,1024,4,1,128]{4,2,3,1,0:T(4,128)(2,1)S(1)}, bf16[1,1024,4,1,128]{4,2,3,1,0:T(4,128)(2,1)}, u32[]{:S(2)}) copy-start(bf16[1,1024,4,1,128]{4,2,3,1,0:T(4,128)(2,1)} %get-tuple-element.38) | copy-start | bytes 3145732
  390.6 9.5 %collective-permute-start.24 = (f32[256,256]{0,1:T(8,128)S(1)}, f32[256,256]{0,1:T(8,128)S(1)}, u32[]{:S(2)}, u32[]{:S(2)}) collective-permute-start(f32[256,256]{0,1:T(8,128)S(1)} %broadcast_select_fusion.3), channel_id=1, source_target_pairs={{0,2},{2,0},{1,3},{3,1},{4,6},{6,4},{5,7},{7,5},{8,10},{10,8},{9,1... | collective-permute-start | bytes 786440 | tf_op jit(solution)/shard_map/ppermute | solution.py:16
  400.2 5.0 %collective-permute-start.25 = (f32[128,256]{0,1:T(8,128)S(1)}, f32[128,256]{0,1:T(8,128)S(1)}, u32[]{:S(2)}, u32[]{:S(2)}) collective-permute-start(f32[128,256]{0,1:T(8,128)S(1)} %slice_select_fusion.3), channel_id=1, source_target_pairs={{0,1},{1,0},{2,3},{3,2},{4,5},{5,4},{6,7},{7,6},{8,9},{9,8},{10,11... | collective-permute-start | bytes 393224 | tf_op jit(solution)/shard_map/ppermute | solution.py:16
  405.3 13.6 %copy-start.13 = (bf16[1,1024,4,1,128]{4,2,3,1,0:T(4,128)(2,1)S(1)}, bf16[1,1024,4,1,128]{4,2,3,1,0:T(4,128)(2,1)}, u32[]{:S(2)}) copy-start(bf16[1,1024,4,1,128]{4,2,3,1,0:T(4,128)(2,1)} %copy-done.12) | copy-start | bytes 3145732
  419.4 9.3 %collective-permute-start.26 = (f32[256,256]{0,1:T(8,128)S(1)}, f32[256,256]{0,1:T(8,128)S(1)}, u32[]{:S(2)}, u32[]{:S(2)}) collective-permute-start(f32[256,256]{0,1:T(8,128)S(1)} %broadcast_select_fusion.2), channel_id=1, source_target_pairs={{0,2},{2,0},{1,3},{3,1},{4,6},{6,4},{5,7},{7,5},{8,10},{10,8},{9,1... | collective-permute-start | bytes 786440 | tf_op jit(solution)/shard_map/ppermute | solution.py:16
  428.8 5.6 %collective-permute-start.27 = (f32[128,256]{0,1:T(8,128)S(1)}, f32[128,256]{0,1:T(8,128)S(1)}, u32[]{:S(2)}, u32[]{:S(2)}) collective-permute-start(f32[128,256]{0,1:T(8,128)S(1)} %slice_select_fusion.2), channel_id=1, source_target_pairs={{0,1},{1,0},{2,3},{3,2},{4,5},{5,4},{6,7},{7,6},{8,9},{9,8},{10,11... | collective-permute-start | bytes 393224 | tf_op jit(solution)/shard_map/ppermute | solution.py:16
  434.4 8.0 %collective-permute-start.28 = (f32[256,256]{0,1:T(8,128)S(1)}, f32[256,256]{0,1:T(8,128)S(1)}, u32[]{:S(2)}, u32[]{:S(2)}) collective-permute-start(f32[256,256]{0,1:T(8,128)S(1)} %pad_maximum_fusion.12), channel_id=1, source_target_pairs={{0,2},{2,0},{1,3},{3,1},{4,6},{6,4},{5,7},{7,5},{8,10},{10,8},{9,1... | collective-permute-start | bytes 786440 | tf_op jit(solution)/shard_map/ppermute | solution.py:16
where the time goes:
time: 454 us; the launch traced here: 445 us
  waiting for transfers between devices  185 us (41%)
  blocking collectives  154 us (34%)
  starting transfers between devices  38.8 us (9%)
  matrix products  28.9 us (6%)
  local copies, waits for them, and re-layouts  25.5 us (6%)
  other arithmetic  11 us (2%)
    ppermute x29, waiting for transfers between devices, partner_2(): return lax.ppermute(block, axis, route)  145 us
    all_to_all x4, blocking collectives, summed_on_arrival(): lax.all_to_all(cut_along(value, dim, peers), axis, 0, 0, tiled=True)  89.4 us
    all_to_all x5, blocking collectives, copy_for_each(): return lax.all_to_all(copies, axis, split_axis=0, concat_axis=0, tiled=True)  64.5 us
    all_to_all x2, waiting for transfers between devices, summed_on_arrival(): lax.all_to_all(cut_along(value, dim, peers), axis, 0, 0, tiled=True)  29.8 us
    ppermute x29, starting transfers between devices, partner_2(): return lax.ppermute(block, axis, route)  28 us
    slice x5, local copies, waits for them, and re-layouts, panel_parts(): return (merged[0], merged[1])  13.7 us
    dot_general x10, matrix products, complex_apply(): lax.dot_general(real_part, right_side, dim_numbers, preferred_element_typ...  13.5 us
    all_to_all x1, waiting for transfers between devices, copy_for_each(): return lax.all_to_all(copies, axis, split_axis=0, concat_axis=0, tiled=True)  10.1 us
  transfers between devices with their start and end apart: 32, of which 31 were waited for; matrix products, arithmetic and copies ran while one was open for 4% of the time, Pallas kernels for 0%

commit v1 on v0

v1 whole, which is shorter than its diff:
```python
import functools

import jax
import jax.numpy as jnp
from jax import lax
from jax.experimental import pallas as pl
from jax.experimental.pallas import tpu as pltpu
from jax.sharding import PartitionSpec as P

BF = jnp.bfloat16
F32 = jnp.float32
B = 128
C = 256
STEPS = (1, 3, 2)
X, Y, Z, CORE, ROW, T0, T1, T2 = range(8)
SMALL = 8 << 20
LARGE = 28 << 20


def swap(value, axis, mask):
    count = lax.axis_size(axis)
    return lax.ppermute(value, axis, [(i, i ^ mask) for i in range(count)])


def small(body, outs, scal, *ins):
    return pl.pallas_call(
        body,
        out_shape=[jax.ShapeDtypeStruct(*o) for o in outs],
        in_specs=[pl.BlockSpec(memory_space=pltpu.SMEM)]
        + [pl.BlockSpec(memory_space=pltpu.VMEM)] * len(ins),
        out_specs=[pl.BlockSpec(memory_space=pltpu.VMEM)] * len(outs),
        compiler_params=pltpu.CompilerParams(vmem_limit_bytes=SMALL),
        cost_estimate=pl.CostEstimate(flops=1 << 18, bytes_accessed=1 << 19, transcendentals=0),
    )(scal, *ins)


def relay_body(groups, real_ref, imag_ref, out_ref):
    span = C // groups
    shift = span.bit_length() - 1
    target = lax.broadcasted_iota(jnp.int32, (C, C), 0)
    source = lax.broadcasted_iota(jnp.int32, (C, C), 1)
    place = (source == (target & span - 1) * groups + (target >> shift)).astype(BF)
    for chunk in range(B * groups // C):
        rows = slice(chunk * C, (chunk + 1) * C)
        both = jnp.concatenate([real_ref[rows, :], imag_ref[rows, :]], axis=1)
        moved = jnp.dot(place, both, preferred_element_type=F32).astype(BF)
        for p in range(groups):
            out_ref[chunk * span : (chunk + 1) * span, p * C : (p + 1) * C] = moved[
                p * span : (p + 1) * span
            ]


def relay(weights):
    _, rows, groups, _, width = weights.shape
    flat = weights.reshape(2 * rows * groups, width)
    tiles = rows // B
    return pl.pallas_call(
        functools.partial(relay_body, groups),
        grid=(tiles,),
        out_shape=jax.ShapeDtypeStruct((rows, groups * C), BF),
        in_specs=[
            pl.BlockSpec((B * groups, B), lambda t: (t, 0)),
            pl.BlockSpec((B * groups, B), lambda t: (t + tiles, 0)),
        ],
        out_specs=pl.BlockSpec((B, groups * C), lambda t: (t, 0)),
        compiler_params=pltpu.CompilerParams(vmem_limit_bytes=LARGE),
        cost_estimate=pl.CostEstimate(
            flops=4 * rows * groups * C * B, bytes_accessed=8 * rows * groups * B, transcendentals=0
        ),
    )(flat, flat)


def forward(weights, scal, ins, gather, extras=()):
    rows, depth = weights.shape
    tiles = rows // C
    count = len(ins)

    def body(s, w_ref, *refs):
        in_refs, own_ref, other_ref = refs[:count], refs[count], refs[count + 1]
        extra_refs = refs[count + 2 : -2]
        vec, acc = refs[-2:]

        @pl.when(pl.program_id(0) == 0)
        def _():
            for index, block in gather(s, in_refs, extra_refs):
                start = pl.multiple_of(index * C, C)
                block = block.astype(F32)
                vec[pl.ds(start, B), :] = block.astype(BF)
                vec[pl.ds(start + B, B), :] = jnp.concatenate(
                    [-block[:, B:], block[:, :B]], axis=1
                ).astype(BF)

        prod = jnp.dot(w_ref[...], vec[...], preferred_element_type=F32)
        acc[0] = prod[:B]
        acc[1] = prod[B:]
        own_ref[0] = acc[s[CORE]]
        other_ref[0] = acc[1 - s[CORE]].astype(BF)

    def whole(shape):
        return pl.BlockSpec(shape, lambda t, s: (0,) * len(shape))

    spread = pl.BlockSpec((1, B, C), lambda t, s: (t ^ s[Z], 0, 0))
    return pl.pallas_call(
        body,
        grid_spec=pltpu.PrefetchScalarGridSpec(
            num_scalar_prefetch=1,
            grid=(tiles,),
            in_specs=[pl.BlockSpec((C, depth), lambda t, s: (t, 0))] + [whole(i.shape) for i in ins],
            out_specs=[spread, spread] + [whole(e) for e in extras],
            scratch_shapes=[pltpu.VMEM((depth, C), BF), pltpu.VMEM((2, B, C), F32)],
        ),
        out_shape=[
            jax.ShapeDtypeStruct((tiles, B, C), F32),
            jax.ShapeDtypeStruct((tiles, B, C), BF),
        ]
        + [jax.ShapeDtypeStruct(e, F32) for e in extras],
        compiler_params=pltpu.CompilerParams(vmem_limit_bytes=LARGE),
        cost_estimate=pl.CostEstimate(
            flops=2 * rows * depth * C, bytes_accessed=2 * rows * depth, transcendentals=0
        ),
    )(scal, weights, *ins)


def transposed(weights, scal, pieces, paired=None):
    rows, depth = weights.shape
    tiles = depth // (4 * C)
    ins = list(pieces.values()) + ([] if paired is None else [paired])
    keys = list(pieces)
    count = len(ins)
    planes = {k: 1 if paired is None else 3 if k == 2 else 2 for k in range(4)}

    def body(s, w_ref, *refs):
        in_refs, out_refs, (vec, acc) = refs[:count], refs[count : count + 4], refs[-2:]

        @pl.when(pl.program_id(0) == 0)
        def _():
            for (zz, j), ref in zip(keys, in_refs):
                slot = 2 * (s[Z] ^ zz) + (s[CORE] ^ j)
                vec[:, pl.ds(pl.multiple_of(slot * B, B), B)] = ref[...]

        prod = jnp.dot(vec[...], w_ref[...], preferred_element_type=F32)
        for p in range(4):
            part = prod[:, p * C : (p + 1) * C]
            acc[p, :B] = part[:B, :B] - part[B:, B:]
            acc[p, B:] = part[B:, :B] + part[:B, B:]
        for k in range(4):
            kind = out_refs[k].dtype
            out_refs[k][0] = acc[s[X] ^ k].astype(kind)
            if paired is not None:
                out_refs[k][1] = acc[s[X] ^ k ^ 2].astype(kind)
                if k == 2:
                    out_refs[k][2] = in_refs[-1][...]

    def out_spec(k):
        if paired is None:
            mask = {4: 3, 2: 1, 1: 0}[tiles]
            return pl.BlockSpec((1, C, B), lambda t, s: (t ^ s[Y] & mask, 0, 0))
        return pl.BlockSpec((planes[k], C, B), lambda t, s: (0, 0, 0))

    return pl.pallas_call(
        body,
        grid_spec=pltpu.PrefetchScalarGridSpec(
            num_scalar_prefetch=1,
            grid=(tiles,),
            in_specs=[pl.BlockSpec((rows, 4 * C), lambda t, s: (0, t))]
            + [pl.BlockSpec((C, B), lambda t, s: (0, 0))] * count,
            out_specs=[out_spec(k) for k in range(4)],
            scratch_shapes=[pltpu.VMEM((C, rows), BF), pltpu.VMEM((4, C, B), F32)],
        ),
        out_shape=[
            jax.ShapeDtypeStruct((tiles * planes[k], C, B), BF if k else F32) for k in range(4)
        ],
        compiler_params=pltpu.CompilerParams(vmem_limit_bytes=LARGE),
        cost_estimate=pl.CostEstimate(
            flops=2 * rows * depth * C, bytes_accessed=2 * rows * depth, transcendentals=0
        ),
    )(scal, weights, *ins)


def same(goal, slot):
    return (goal == slot.astype(F32)).astype(F32)


def shards(leaf_update, rhs, inv_top, inv_mid, inv_low, couple_mid, couple_low, block_map):
    leaf = lax.axis_index("leaf")
    row = lax.axis_index("row")
    scal = jnp.concatenate(
        [jnp.stack([leaf & 3, leaf >> 2, row >> 1, row & 1, row]).astype(jnp.int32), block_map[:, 0]]
    )

    def reduce_row(own, other, tail, outs, *ins):
        other = swap(other, "row", 1)

        def split(s, own_ref, other_ref, *out_refs):
            for k, ref in enumerate(out_refs):
                ref[...] = (own_ref[k] + other_ref[k].astype(F32)).astype(ref.dtype)

        parts = small(
            split, [((B, C), F32)] + [((B, C), BF)] * 3, scal, own, other
        )
        got = [swap(parts[k], "row", 2 * k) for k in STEPS]

        def body(s, *refs):
            total = refs[0][...]
            for ref in refs[1:4]:
                total = total + ref[...].astype(F32)
            tail(s, total, *refs[4:])

        return small(body, outs, scal, parts[0], *got, *ins)

    def gather_row(own):
        pieces = {(0, 0): own}
        for k in STEPS:
            pieces[(k, 0)] = swap(own, "row", 2 * k)
        for k in (0,) + STEPS:
            pieces[(k, 1)] = swap(pieces[(k, 0)], "row", 1)
        return pieces

    def gather_x(value):
        return [value] + [swap(value, "leaf", k) for k in (1, 2, 3)]

    def send(s, leaf_ref, rhs_ref, low_ref, y1_ref, y3_ref):
        def tag(level):
            return jnp.full((16, C), s[T0 + level].astype(F32), F32).astype(BF)

        low_ref[:B] = leaf_ref[...].astype(BF)
        low_ref[B : 2 * B] = rhs_ref[2].astype(BF)
        low_ref[2 * B :] = tag(2)
        y1_ref[:B] = rhs_ref[1].astype(BF)
        y1_ref[B : 2 * B] = rhs_ref[0].astype(BF)
        y1_ref[2 * B : 2 * B + 16] = tag(1)
        y1_ref[2 * B + 16 :] = tag(0)
        y3_ref[:B] = rhs_ref[0].astype(BF)
        y3_ref[B:] = tag(0)

    low, to_y1, to_y3 = small(
        send,
        [((2 * B + 16, C), BF), ((2 * B + 32, C), BF), ((B + 16, C), BF)],
        scal,
        leaf_update,
        rhs,
    )
    got = gather_x(low)
    from_y1 = swap(to_y1, "leaf", 4)
    from_y3 = swap(to_y3, "leaf", 12)
    from_y2 = swap(to_y3, "leaf", 8)
    w_low, b_low, w_mid, b_mid, w_top = [
        relay(w) for w in (inv_low, couple_low, inv_mid, couple_mid, inv_top)
    ]

    def gather_low(s, refs, extra):
        goal = [r[2 * B : 2 * B + 16, :].astype(F32)[:1] for r in refs]
        child = [r[:B, :].astype(F32) for r in refs]
        slot = (s[X] + 4) * 8 + s[ROW]
        extra[0][...] = same(goal[0], slot) * child[0] + same(goal[2], slot) * child[2]
        for k in range(4):
            slot = (s[X] ^ k) * 8 + s[ROW]
            yield s[X] ^ k, (
                refs[k][B : 2 * B, :].astype(F32)
                + same(goal[k], slot) * child[k]
                + same(goal[k ^ 2], slot) * child[k ^ 2]
            )

    own, other, update = forward(w_low, scal, got, gather_low, [(B, C)])

    def keep(s, total, full_ref, half_ref):
        full_ref[...] = total
        half_ref[...] = total.astype(BF)

    pair_outs = [((B, C), F32), ((B, C), BF)]
    y_low, half = reduce_row(own, other, keep, pair_outs)

    def gather_plain(s, refs, extra):
        for k in range(4):
            yield s[X] ^ k, refs[k][...]

    own, other = forward(b_low, scal, gather_x(half), gather_plain)

    def less(s, total, up_ref, full_ref, half_ref):
        keep(s, up_ref[...] - total, full_ref, half_ref)

    children, half = reduce_row(own, other, less, pair_outs, update)

    theirs = swap(half, "leaf", 4)

    def extend_mid(s, own_ref, other_ref, rhs_ref, y1_ref, pair_ref, up_ref):
        position = (s[Y] & 1) * 4 + s[X]
        goal_own = jnp.full((1, C), s[T1].astype(F32), F32)
        goal_other = y1_ref[2 * B : 2 * B + 16, :].astype(F32)[:1]

        def landed(slot):
            return same(goal_own, slot) * own_ref[...] + same(goal_other, slot) * other_ref[
                ...
            ].astype(F32)

        slot = position * 8 + s[ROW]
        pair_ref[0] = (rhs_ref[1] + landed(slot)).astype(BF)
        up_ref[...] = landed(slot + 64)
        slot = (position ^ 4) * 8 + s[ROW]
        pair_ref[1] = (y1_ref[:B, :].astype(F32) + landed(slot)).astype(BF)

    pair, update = small(
        extend_mid, [((2, B, C), BF), ((B, C), F32)], scal, children, theirs, rhs, from_y1
    )

    def gather_mid(s, refs, extra):
        for k in range(4):
            for j in range(2):
                yield ((s[Y] & 1) ^ j) * 4 + (s[X] ^ k), refs[k][j]

    own, other = forward(w_mid, scal, gather_x(pair), gather_mid)
    y_mid, half = reduce_row(own, other, keep, pair_outs)

    def join(s, a_ref, b_ref, out_ref):
        out_ref[0] = a_ref[...]
        out_ref[1] = b_ref[...]

    (pair,) = small(join, [((2, B, C), BF)], scal, half, swap(half, "leaf", 4))
    own, other = forward(b_mid, scal, gather_x(pair), gather_mid)
    children, half = reduce_row(own, other, less, pair_outs, update)

    moved = [swap(half, "leaf", 4 * k) for k in STEPS]

    def extend_top(s, own_ref, m1, m3, m2, rhs_ref, y1_ref, y3_ref, y2_ref, out_ref):
        child = [own_ref[...], m1[...].astype(F32), m2[...].astype(F32), m3[...].astype(F32)]
        base = [rhs_ref[0], y1_ref[B : 2 * B, :], y2_ref[:B, :], y3_ref[:B, :]]
        goal = [
            jnp.full((1, C), s[T0].astype(F32), F32),
            y1_ref[2 * B + 16 : 2 * B + 32, :].astype(F32)[:1],
            y2_ref[B : B + 16, :].astype(F32)[:1],
            y3_ref[B : B + 16, :].astype(F32)[:1],
        ]
        for k in range(4):
            slot = ((s[Y] ^ k) * 4 + s[X]) * 8 + s[ROW]
            out_ref[k] = (
                base[k].astype(F32)
                + same(goal[k], slot) * child[k]
                + same(goal[k ^ 2], slot) * child[k ^ 2]
            ).astype(BF)

    (column,) = small(
        extend_top, [((4, B, C), BF)], scal, children, *moved, rhs, from_y1, from_y3, from_y2
    )

    def gather_top(s, refs, extra):
        for k in range(4):
            for j in range(4):
                yield (s[Y] ^ j) * 4 + (s[X] ^ k), refs[k][j]

    own, other = forward(w_top, scal, gather_x(column), gather_top)

    def turn(s, total, out_ref):
        out_ref[...] = total.T.astype(BF)

    turned = [((C, B), BF)]
    (half,) = reduce_row(own, other, turn, turned)
    parts = transposed(w_top, scal, gather_row(half))
    got = [swap(parts[k], "leaf", k) for k in STEPS]

    def sum_top(s, own_ref, a, b, c, pair_ref, m1, m3, m2):
        total = [
            own_ref[j] + a[j].astype(F32) + b[j].astype(F32) + c[j].astype(F32) for j in range(4)
        ]
        pair_ref[0] = total[0]
        pair_ref[1] = total[2]
        for k, ref in zip(STEPS, (m1, m3, m2)):
            ref[0] = total[k].astype(BF)
            ref[1] = total[k ^ 2].astype(BF)

    pair, *sent = small(
        sum_top, [((2, C, B), F32)] + [((2, C, B), BF)] * 3, scal, parts[0], *got
    )
    got = [swap(m, "leaf", 4 * k) for k, m in zip(STEPS, sent)]

    def end_top(s, pair_ref, a, b, c, x_ref, down_ref, half_ref):
        own, other = [
            pair_ref[j] + a[j].astype(F32) + b[j].astype(F32) + c[j].astype(F32) for j in range(2)
        ]
        x_ref[...] = own
        position = s[Y] * 4 + s[X]
        hit = same(jnp.full((1, B), s[T0].astype(F32), F32), position * 8 + s[ROW])
        down = own * hit + other * (1.0 - hit)
        down_ref[...] = down
        half_ref[...] = down.astype(BF)

    x_top, down_mid, half = small(
        end_top, [((C, B), F32), ((C, B), F32), ((C, B), BF)], scal, pair, *got
    )

    down_half = half
    parts = transposed(b_mid, scal, gather_row(half))
    got = [swap(parts[k], "leaf", k) for k in STEPS]

    def sum_mid(s, own_ref, a, b, c, full_ref, half_ref):
        total = [
            own_ref[j] + a[j].astype(F32) + b[j].astype(F32) + c[j].astype(F32) for j in range(2)
        ]
        full_ref[...] = total[0]
        half_ref[...] = total[1].astype(BF)

    full, half = small(sum_mid, [((C, B), F32), ((C, B), BF)], scal, parts[0], *got)

    def reduced_mid(s, y_ref, full_ref, got_ref, out_ref):
        out_ref[...] = (y_ref[...].T - (full_ref[...] + got_ref[...].astype(F32))).astype(BF)

    (half,) = small(reduced_mid, turned, scal, y_mid, full, swap(half, "leaf", 4))
    parts = transposed(w_mid, scal, gather_row(half))
    got = [swap(parts[k], "leaf", k) for k in STEPS]

    def pair_mid(s, own_ref, a, b, c, down_ref, full_ref, out_ref):
        for j in range(2):
            total = own_ref[j] + a[j].astype(F32) + b[j].astype(F32) + c[j].astype(F32)
            full_ref[j] = total
            out_ref[1 - j] = total.astype(BF)
        out_ref[2] = down_ref[...]

    full, sent = small(
        pair_mid, [((2, C, B), F32), ((3, C, B), BF)], scal, parts[0], *got, down_half
    )

    def choose(s, target, base, blocks):
        down = None
        goal = jnp.full((1, B), target.astype(F32), F32)
        for slot, block in zip(base, blocks):
            term = block * same(goal, slot)
            down = term if down is None else down + term
        return down

    def end_mid(s, full_ref, got_ref, down_ref, x_ref, out_ref, half_ref):
        own = full_ref[0] + got_ref[0].astype(F32)
        other = full_ref[1] + got_ref[1].astype(F32)
        x_ref[...] = own
        position = (s[Y] & 1) * 4 + s[X]
        slot, far = position * 8 + s[ROW], (position ^ 4) * 8 + s[ROW]
        down = choose(
            s,
            s[T1],
            (slot, slot + 64, far, far + 64),
            (own, down_ref[...], other, got_ref[2].astype(F32)),
        )
        out_ref[...] = down
        half_ref[...] = down.astype(BF)

    x_mid, down_low, half = small(
        end_mid,
        [((C, B), F32), ((C, B), F32), ((C, B), BF)],
        scal,
        full,
        swap(sent, "leaf", 4),
        down_mid,
    )

    down_half = half
    parts = transposed(b_low, scal, gather_row(half))
    got = [swap(parts[k], "leaf", k) for k in STEPS]

    def reduced_low(s, y_ref, own_ref, a, b, c, out_ref):
        total = own_ref[0] + a[0].astype(F32) + b[0].astype(F32) + c[0].astype(F32)
        out_ref[...] = (y_ref[...].T - total).astype(BF)

    (half,) = small(reduced_low, turned, scal, y_low, parts[0], *got)
    parts = transposed(w_low, scal, gather_row(half), down_half)
    got = [swap(parts[k], "leaf", k) for k in STEPS]

    def end_low(s, own_ref, a, b, c, down_ref, top_ref, mid_ref, sol_ref, leaf_ref):
        own, other = [
            own_ref[j] + a[j].astype(F32) + b[j].astype(F32) + c[j].astype(F32) for j in range(2)
        ]
        sol_ref[0] = top_ref[...].T
        sol_ref[1] = mid_ref[...].T
        sol_ref[2] = own.T
        slot, far = s[X] * 8 + s[ROW], (s[X] ^ 2) * 8 + s[ROW]
        leaf_ref[...] = choose(
            s,
            s[T2],
            (slot, slot + 32, far, far + 32),
            (own, down_ref[...], other, c[2].astype(F32)),
        ).T

    solved, leaf_solution = small(
        end_low,
        [((3, B, C), F32), ((B, C), F32)],
        scal,
        parts[0],
        *got,
        down_low,
        x_top,
        x_mid,
    )
    return (solved, leaf_solution)


def solution(mesh):
    return jax.shard_map(
        shards,
        mesh=mesh,
        in_specs=(
            P(("leaf", "row"), None),
            P(None, ("leaf", "row"), None),
            P(None, "leaf", None, "row", None),
            P(None, "leaf", None, "row", None),
            P(None, "leaf", None, "row", None),
            P(None, "leaf", None, "row", None),
            P(None, "leaf", None, "row", None),
            P(None, ("leaf", "row")),
        ),
        out_specs=(P(None, ("leaf", "row"), None), P(("leaf", "row"), None)),
        check_vma=False,
    )
```

time: 454 us -> 279 us (0.61); the launches traced: 445 us -> 278 us
  blocking collectives: 154 us -> 0 us
  waiting for transfers between devices: 185 us -> 119 us
  starting transfers between devices: 38.8 us -> 102 us
  Pallas kernels: 0 us -> 51.8 us
  matrix products: 28.9 us -> 0 us
  local copies, waits for them, and re-layouts: 25.5 us -> 4.25 us
  other arithmetic: 11 us -> 0.01 us
    all_to_all x9 -> x0, blocking collectives: 154 us -> none  [the longest x4 89.4 us: summed_on_arrival(): lax.all_to_all(cut_along(value, dim, peers), axis, 0, 0, tiled=True)]
    ppermute x29 -> x98, starting transfers between devices: 28 us -> 102 us  [swap(): return lax.ppermute(value, axis, [(i, i ^ mask) for i in range(count)])]
    pallas_call x0 -> x37, Pallas kernels: none -> 51.8 us  [the longest x22 14.2 us: small(): pl.pallas_call(body, out_shape=[jax.ShapeDtypeStruct(*o) for o in outs],...]
    all_to_all x3 -> x0, waiting for transfers between devices: 39.9 us -> none  [the longest x2 29.8 us: summed_on_arrival(): lax.all_to_all(cut_along(value, dim, peers), axis, 0, 0, tiled=True)]
    dot_general x26 -> x0, matrix products: 28.9 us -> none  [the longest x10 13.5 us: complex_apply(): lax.dot_general(real_part, right_side, dim_numbers, preferred_element_typ...]
    ppermute x29 -> x98, waiting for transfers between devices: 145 us -> 119 us  [swap(): return lax.ppermute(value, axis, [(i, i ^ mask) for i in range(count)])]
    slice x17 -> x0, local copies, waits for them, and re-layouts: 17.9 us -> none  [the longest x5 13.7 us: panel_parts(): return (merged[0], merged[1])]
    all_to_all x3 -> x0, starting transfers between devices: 10.8 us -> none  [the longest x2 7.11 us: summed_on_arrival(): lax.all_to_all(cut_along(value, dim, peers), axis, 0, 0, tiled=True)]
  transfers between devices with their start and end apart: 32 -> 98, of which waited for: 31 -> 67; matrix products, arithmetic and copies ran while one was open for 4% -> 0% of each run, Pallas kernels for 0% -> 5%
where the time goes in v1:
time: 279 us; the launch traced here: 278 us
  waiting for transfers between devices  119 us (43%)
  starting transfers between devices  102 us (37%)
  Pallas kernels  51.8 us (19%)
  local copies, waits for them, and re-layouts  4.25 us (2%)
    ppermute x98, waiting for transfers between devices, swap(): return lax.ppermute(value, axis, [(i, i ^ mask) for i in range(count)])  119 us
    ppermute x98, starting transfers between devices, swap(): return lax.ppermute(value, axis, [(i, i ^ mask) for i in range(count)])  102 us
    pallas_call x22, Pallas kernels, small(): pl.pallas_call(body, out_shape=[jax.ShapeDtypeStruct(*o) for o in outs],...  14.2 us
    pallas_call x5, Pallas kernels, forward(): pl.pallas_call(body, grid_spec=pltpu.PrefetchScalarGridSpec(num_scalar_pr...  12.8 us
    pallas_call x5, Pallas kernels, relay(): pl.pallas_call(functools.partial(relay_body, groups), grid=(tiles,), out_...  12.5 us
    pallas_call x5, Pallas kernels, transposed(): pl.pallas_call(body, grid_spec=pltpu.PrefetchScalarGridSpec(num_scalar_pr...  12.3 us
  transfers between devices with their start and end apart: 98, of which 67 were waited for; matrix products, arithmetic and copies ran while one was open for 0% of the time, Pallas kernels for 5%

profile of v1, /device:TPU:0, one launch (start us, length us, event | category | flops | bytes accessed | tf_op | source)
XLA Modules:
  0.0 278.3 jit_solution(7701657974076053233)
XLA Ops:
  3.9 2.9 %collective-permute-start.2 = (bf16[272,256]{1,0:T(8,128)(2,1)S(1)}, bf16[272,256]{1,0:T(8,128)(2,1)S(1)}, u32[]{:S(2)}, u32[]{:S(2)}) collective-permute-start(bf16[272,256]{1,0:T(8,128)(2,1)S(1)} %get-tuple-element.80.refs_0_), channel_id=1, source_target_pairs={{0,3},{1,2},{2,1},{3,0},{4,7},{5,6},{6,5},{7,4},{8,11},{9,10},{10,... | collective-permute-start | bytes 417800 | tf_op jit(solution)/shard_map/ppermute | solution.py:22
  9.6 1.9 shard_map.95.w_ref
  12.7 2.2 collective-permute-done.1.refs_2_
  14.9 2.1 shard_map.97
  19.2 2.0 collective-permute-start.4
  21.2 2.5 collective-permute-start.5
  24.8 1.9 collective-permute-done.5.refs_2_
  26.7 2.8 %collective-permute-done.6.refs_3_ = bf16[128,256]{1,0:T(8,128)(2,1)S(1)} collective-permute-done((bf16[128,256]{1,0:T(8,128)(2,1)S(1)}, bf16[128,256]{1,0:T(8,128)(2,1)S(1)}, u32[]{:S(2)}, u32[]{:S(2)}) %collective-permute-start.6) | collective-permute-done | bytes 65568 | tf_op jit(solution)/shard_map/ppermute | solution.py:22
  30.1 2.2 collective-permute-start.9
  34.2 1.9 shard_map.100.w_ref
  36.2 1.8 collective-permute-done.8.refs_2_
  38.0 1.9 shard_map.102
  44.0 2.5 collective-permute-start.13
  46.7 3.2 %collective-permute-done.12.refs_2_ = bf16[128,256]{1,0:T(8,128)(2,1)S(1)} collective-permute-done((bf16[128,256]{1,0:T(8,128)(2,1)S(1)}, bf16[128,256]{1,0:T(8,128)(2,1)S(1)}, u32[]{:S(2)}, u32[]{:S(2)}) %collective-permute-start.12) | collective-permute-done | bytes 65568 | tf_op jit(solution)/shard_map/ppermute | solution.py:22
  52.0 2.8 %collective-permute-done.14.other_ref = bf16[128,256]{1,0:T(8,128)(2,1)S(1)} collective-permute-done((bf16[128,256]{1,0:T(8,128)(2,1)S(1)}, bf16[128,256]{1,0:T(8,128)(2,1)S(1)}, u32[]{:S(2)}, u32[]{:S(2)}) %collective-permute-start.14) | collective-permute-done | bytes 65568 | tf_op jit(solution)/shard_map/ppermute | solution.py:22
  59.7 2.5 shard_map.101.w_ref
  64.0 2.5 shard_map.106
  69.3 2.5 collective-permute-start.21
  74.7 2.8 %collective-permute-done.22.refs_3_ = bf16[128,256]{1,0:T(8,128)(2,1)S(1)} collective-permute-done((bf16[128,256]{1,0:T(8,128)(2,1)S(1)}, bf16[128,256]{1,0:T(8,128)(2,1)S(1)}, u32[]{:S(2)}, u32[]{:S(2)}) %collective-permute-start.22) | collective-permute-done | bytes 65568 | tf_op jit(solution)/shard_map/ppermute | solution.py:22
  79.6 2.8 %collective-permute-done.23.b_ref = bf16[128,256]{1,0:T(8,128)(2,1)S(1)} collective-permute-done((bf16[128,256]{1,0:T(8,128)(2,1)S(1)}, bf16[128,256]{1,0:T(8,128)(2,1)S(1)}, u32[]{:S(2)}, u32[]{:S(2)}) %collective-permute-start.23) | collective-permute-done | bytes 65568 | tf_op jit(solution)/shard_map/ppermute | solution.py:22
  87.2 2.5 shard_map.109.w_ref
  91.5 2.5 shard_map.112
  98.1 2.4 collective-permute-start.30
  100.5 3.1 %collective-permute-start.35 = (bf16[144,256]{1,0:T(8,128)(2,1)S(1)}, bf16[144,256]{1,0:T(8,128)(2,1)S(1)}, u32[]{:S(2)}, u32[]{:S(2)}) collective-permute-start(bf16[144,256]{1,0:T(8,128)(2,1)S(1)} %get-tuple-element.117), channel_id=1, source_target_pairs={{0,8},{1,9},{2,10},{3,11},{4,12},{5,13},{6,14},{7,15},{8,0},{9,1},... | collective-permute-start | bytes 221192 | tf_op jit(solution)/shard_map/ppermute | solution.py:22
  105.2 2.4 collective-permute-start.33
  109.6 1.8 collective-permute-done.33.m2
  111.4 1.7 collective-permute-done.32.m3
  118.0 3.6 %shard_map.110.w_ref = bf16[1024,4096]{1,0:T(8,128)(2,1)S(1)} custom-call(bf16[32768,128]{1,0:T(8,128)(2,1)S(1)} %bitcast.13, bf16[32768,128]{1,0:T(8,128)(2,1)S(1)} %bitcast.14), custom_call_target="tpu_custom_call" | custom-call | flops 2147483648 | bytes 16777216 | tf_op jit(solution)/shard_map/pallas_call | solution.py:57
  121.6 4.4 %collective-permute-done.38.refs_3_ = bf16[4,128,256]{2,1,0:T(8,128)(2,1)S(1)} collective-permute-done((bf16[4,128,256]{2,1,0:T(8,128)(2,1)S(1)}, bf16[4,128,256]{2,1,0:T(8,128)(2,1)S(1)}, u32[]{:S(2)}, u32[]{:S(2)}) %collective-permute-start.38) | collective-permute-done | bytes 262176 | tf_op jit(solution)/shard_map/ppermute | solution.py:22
  126.6 3.7 %shard_map.116 = (f32[4,128,256]{2,1,0:T(8,128)S(1)}, bf16[4,128,256]{2,1,0:T(8,128)(2,1)S(1)}) custom-call(s32[8]{0:T(128)S(1)} %concatenate.3.s, bf16[1024,4096]{1,0:T(8,128)(2,1)S(1)} %shard_map.110.w_ref, bf16[4,128,256]{2,1,0:T(8,128)(2,1)S(1)} %shard_map.115.refs_0_, bf16[4,128,256]{2,1,0:T(8,128)(2,1)S(1)} %collective-permute-done.36.refs_1_, ...), custom_call_target="tpu_custom_call" | custom-call | flops 2147483648 | bytes 8388608 | tf_op jit(solution)/shard_map/pallas_call | solution.py:103
  133.6 2.6 collective-permute-start.41
  137.2 1.8 collective-permute-done.41.refs_2_
  139.1 2.9 %collective-permute-done.42.refs_3_ = bf16[128,256]{1,0:T(8,128)(2,1)S(1)} collective-permute-done((bf16[128,256]{1,0:T(8,128)(2,1)S(1)}, bf16[128,256]{1,0:T(8,128)(2,1)S(1)}, u32[]{:S(2)}, u32[]{:S(2)}) %collective-permute-start.42) | collective-permute-done | bytes 65568 | tf_op jit(solution)/shard_map/ppermute | solution.py:22
  143.7 2.6 collective-permute-start.44
  146.4 2.3 collective-permute-done.45.refs_3_
  151.9 4.3 %shard_map.119 = (f32[4,256,128]{2,1,0:T(8,128)S(1)}, bf16[4,256,128]{2,1,0:T(8,128)(2,1)S(1)}, bf16[4,256,128]{2,1,0:T(8,128)(2,1)S(1)}, bf16[4,256,128]{2,1,0:T(8,128)(2,1)S(1)}) custom-call(s32[8]{0:T(128)S(1)} %concatenate.3.s, bf16[1024,4096]{1,0:T(8,128)(2,1)S(1)} %shard_map.110.w_ref, bf16[256,128]{1,0:T(8,128)(2,1)S(1)} %shard_map.118.refs_0_, ...), custom_call_target="tpu_custom_call" | custom-call | flops 2147483648 | bytes 8388608 | tf_op jit(solution)/shard_map/pallas_call | solution.py:160
  156.9 2.0 collective-permute-start.51
  160.4 5.1 %collective-permute-done.50.a = bf16[4,256,128]{2,1,0:T(8,128)(2,1)S(1)} collective-permute-done((bf16[4,256,128]{2,1,0:T(8,128)(2,1)S(1)}, bf16[4,256,128]{2,1,0:T(8,128)(2,1)S(1)}, u32[]{:S(2)}, u32[]{:S(2)}) %collective-permute-start.50) | collective-permute-done | bytes 262176 | tf_op jit(solution)/shard_map/ppermute | solution.py:22
  165.5 6.4 %collective-permute-done.51.b = bf16[4,256,128]{2,1,0:T(8,128)(2,1)S(1)} collective-permute-done((bf16[4,256,128]{2,1,0:T(8,128)(2,1)S(1)}, bf16[4,256,128]{2,1,0:T(8,128)(2,1)S(1)}, u32[]{:S(2)}, u32[]{:S(2)}) %collective-permute-start.51) | collective-permute-done | bytes 262176 | tf_op jit(solution)/shard_map/ppermute | solution.py:22
  174.1 2.6 collective-permute-start.55
  176.7 1.8 collective-permute-done.53.a
  178.5 2.4 collective-permute-done.54.b
  185.1 2.3 collective-permute-done.58.refs_3_
  189.8 2.5 shard_map.122
  194.6 1.9 collective-permute-start.65
  196.5 2.1 collective-permute-done.63.a
  198.7 3.7 %collective-permute-done.64.b = bf16[2,256,128]{2,1,0:T(8,128)(2,1)S(1)} collective-permute-done((bf16[2,256,128]{2,1,0:T(8,128)(2,1)S(1)}, bf16[2,256,128]{2,1,0:T(8,128)(2,1)S(1)}, u32[]{:S(2)}, u32[]{:S(2)}) %collective-permute-start.64) | collective-permute-done | bytes 131104 | tf_op jit(solution)/shard_map/ppermute | solution.py:22
  204.1 3.2 %collective-permute-done.66.got_ref = bf16[256,128]{1,0:T(8,128)(2,1)S(1)} collective-permute-done((bf16[256,128]{1,0:T(8,128)(2,1)S(1)}, bf16[256,128]{1,0:T(8,128)(2,1)S(1)}, u32[]{:S(2)}, u32[]{:S(2)}) %collective-permute-start.66) | collective-permute-done | bytes 65568 | tf_op jit(solution)/shard_map/ppermute | solution.py:22
  207.9 2.1 collective-permute-start.69
  211.5 2.7 collective-permute-done.69.refs_3_
  217.0 2.5 shard_map.125
  219.9 1.8 collective-permute-start.75
  221.7 2.0 collective-permute-start.76
  223.7 2.2 collective-permute-done.74.a
  227.6 1.8 collective-permute-done.76.c
  231.1 5.2 %collective-permute-done.77.got_ref = bf16[3,256,128]{2,1,0:T(8,128)(2,1)S(1)} collective-permute-done((bf16[3,256,128]{2,1,0:T(8,128)(2,1)S(1)}, bf16[3,256,128]{2,1,0:T(8,128)(2,1)S(1)}, u32[]{:S(2)}, u32[]{:S(2)}) %collective-permute-start.77) | collective-permute-done | bytes 196640 | tf_op jit(solution)/shard_map/ppermute | solution.py:22
  240.5 2.3 collective-permute-done.80.refs_3_
  246.6 1.8 collective-permute-start.86
  248.5 2.2 collective-permute-start.87
  252.2 2.0 collective-permute-done.87.c
  254.9 2.0 collective-permute-start.90
  258.5 3.0 %collective-permute-done.90.refs_3_ = bf16[256,128]{1,0:T(8,128)(2,1)S(1)} collective-permute-done((bf16[256,128]{1,0:T(8,128)(2,1)S(1)}, bf16[256,128]{1,0:T(8,128)(2,1)S(1)}, u32[]{:S(2)}, u32[]{:S(2)}) %collective-permute-start.90) | collective-permute-done | bytes 65568 | tf_op jit(solution)/shard_map/ppermute | solution.py:22
  265.4 2.4 collective-permute-start.97
  269.6 6.1 %collective-permute-done.95.a = bf16[2,256,128]{2,1,0:T(8,128)(2,1)S(1)} collective-permute-done((bf16[2,256,128]{2,1,0:T(8,128)(2,1)S(1)}, bf16[2,256,128]{2,1,0:T(8,128)(2,1)S(1)}, u32[]{:S(2)}, u32[]{:S(2)}) %collective-permute-start.95) | collective-permute-done | bytes 131104 | tf_op jit(solution)/shard_map/ppermute | solution.py:22
  (189 shorter events, 106.2 us)
Async XLA Ops:
  3.9 8.9 %collective-permute-start.2 = (bf16[272,256]{1,0:T(8,128)(2,1)S(1)}, bf16[272,256]{1,0:T(8,128)(2,1)S(1)}, u32[]{:S(2)}, u32[]{:S(2)}) collective-permute-start(bf16[272,256]{1,0:T(8,128)(2,1)S(1)} %get-tuple-element.80.refs_0_), channel_id=1, source_target_pairs={{0,3},{1,2},{2,1},{3,0},{4,7},{5,6},{6,5},{7,4},{8,11},{9,10},{10,... | collective-permute-start | bytes 417800 | tf_op jit(solution)/shard_map/ppermute | solution.py:22
  6.8 8.1 %collective-permute-start.1 = (bf16[272,256]{1,0:T(8,128)(2,1)S(1)}, bf16[272,256]{1,0:T(8,128)(2,1)S(1)}, u32[]{:S(2)}, u32[]{:S(2)}) collective-permute-start(bf16[272,256]{1,0:T(8,128)(2,1)S(1)} %get-tuple-element.80.refs_0_), channel_id=1, source_target_pairs={{0,2},{1,3},{2,0},{3,1},{4,6},{5,7},{6,4},{7,5},{8,10},{9,11},{10,... | collective-permute-start | bytes 417800 | tf_op jit(solution)/shard_map/ppermute | solution.py:22
  7.6 7.3 %collective-permute-start = (bf16[272,256]{1,0:T(8,128)(2,1)S(1)}, bf16[272,256]{1,0:T(8,128)(2,1)S(1)}, u32[]{:S(2)}, u32[]{:S(2)}) collective-permute-start(bf16[272,256]{1,0:T(8,128)(2,1)S(1)} %get-tuple-element.80.refs_0_), channel_id=1, source_target_pairs={{0,1},{1,0},{2,3},{3,2},{4,5},{5,4},{6,7},{7,6},{8,9},{9,8},{10,11... | collective-permute-start | bytes 417800 | tf_op jit(solution)/shard_map/ppermute | solution.py:22
  19.2 5.6 %collective-permute-start.4 = (bf16[128,256]{1,0:T(8,128)(2,1)S(1)}, bf16[128,256]{1,0:T(8,128)(2,1)S(1)}, u32[]{:S(2)}, u32[]{:S(2)}) collective-permute-start(bf16[128,256]{1,0:T(8,128)(2,1)S(1)} %get-tuple-element.84), channel_id=1, source_target_pairs={{0,32},{16,48},{32,0},{48,16},{64,96},{80,112},{96,64},{112,80},{1... | collective-permute-start | bytes 196616 | tf_op jit(solution)/shard_map/ppermute | solution.py:22
  21.2 5.5 %collective-permute-start.5 = (bf16[128,256]{1,0:T(8,128)(2,1)S(1)}, bf16[128,256]{1,0:T(8,128)(2,1)S(1)}, u32[]{:S(2)}, u32[]{:S(2)}) collective-permute-start(bf16[128,256]{1,0:T(8,128)(2,1)S(1)} %get-tuple-element.85), channel_id=1, source_target_pairs={{0,96},{16,112},{32,64},{48,80},{64,32},{80,48},{96,0},{112,16},{1... | collective-permute-start | bytes 196616 | tf_op jit(solution)/shard_map/ppermute | solution.py:22
  23.7 5.8 %collective-permute-start.6 = (bf16[128,256]{1,0:T(8,128)(2,1)S(1)}, bf16[128,256]{1,0:T(8,128)(2,1)S(1)}, u32[]{:S(2)}, u32[]{:S(2)}) collective-permute-start(bf16[128,256]{1,0:T(8,128)(2,1)S(1)} %get-tuple-element.86), channel_id=1, source_target_pairs={{0,64},{16,80},{32,96},{48,112},{64,0},{80,16},{96,32},{112,48},{1... | collective-permute-start | bytes 196616 | tf_op jit(solution)/shard_map/ppermute | solution.py:22
  30.1 6.1 %collective-permute-start.9 = (bf16[128,256]{1,0:T(8,128)(2,1)S(1)}, bf16[128,256]{1,0:T(8,128)(2,1)S(1)}, u32[]{:S(2)}, u32[]{:S(2)}) collective-permute-start(bf16[128,256]{1,0:T(8,128)(2,1)S(1)} %get-tuple-element.88.refs_0_), channel_id=1, source_target_pairs={{0,3},{1,2},{2,1},{3,0},{4,7},{5,6},{6,5},{7,4},{8,11},{9,10},{10,... | collective-permute-start | bytes 196616 | tf_op jit(solution)/shard_map/ppermute | solution.py:22
  32.3 5.8 %collective-permute-start.8 = (bf16[128,256]{1,0:T(8,128)(2,1)S(1)}, bf16[128,256]{1,0:T(8,128)(2,1)S(1)}, u32[]{:S(2)}, u32[]{:S(2)}) collective-permute-start(bf16[128,256]{1,0:T(8,128)(2,1)S(1)} %get-tuple-element.88.refs_0_), channel_id=1, source_target_pairs={{0,2},{1,3},{2,0},{3,1},{4,6},{5,7},{6,4},{7,5},{8,10},{9,11},{10,... | collective-permute-start | bytes 196616 | tf_op jit(solution)/shard_map/ppermute | solution.py:22
  33.1 5.0 %collective-permute-start.7 = (bf16[128,256]{1,0:T(8,128)(2,1)S(1)}, bf16[128,256]{1,0:T(8,128)(2,1)S(1)}, u32[]{:S(2)}, u32[]{:S(2)}) collective-permute-start(bf16[128,256]{1,0:T(8,128)(2,1)S(1)} %get-tuple-element.88.refs_0_), channel_id=1, source_target_pairs={{0,1},{1,0},{2,3},{3,2},{4,5},{5,4},{6,7},{7,6},{8,9},{9,8},{10,11... | collective-permute-start | bytes 196616 | tf_op jit(solution)/shard_map/ppermute | solution.py:22
  40.1 11.9 %collective-permute-start.15 = (bf16[288,256]{1,0:T(8,128)(2,1)S(1)}, bf16[288,256]{1,0:T(8,128)(2,1)S(1)}, u32[]{:S(2)}, u32[]{:S(2)}) collective-permute-start(bf16[288,256]{1,0:T(8,128)(2,1)S(1)} %get-tuple-element.98), channel_id=1, source_target_pairs={{0,4},{1,5},{2,6},{3,7},{4,0},{5,1},{6,2},{7,3},{8,12},{9,13},{10,... | collective-permute-start | bytes 442376 | tf_op jit(solution)/shard_map/ppermute | solution.py:22
  43.4 6.5 %collective-permute-start.12 = (bf16[128,256]{1,0:T(8,128)(2,1)S(1)}, bf16[128,256]{1,0:T(8,128)(2,1)S(1)}, u32[]{:S(2)}, u32[]{:S(2)}) collective-permute-start(bf16[128,256]{1,0:T(8,128)(2,1)S(1)} %get-tuple-element.93), channel_id=1, source_target_pairs={{0,96},{16,112},{32,64},{48,80},{64,32},{80,48},{96,0},{112,16},{1... | collective-permute-start | bytes 196616 | tf_op jit(solution)/shard_map/ppermute | solution.py:22
  44.0 5.9 %collective-permute-start.13 = (bf16[128,256]{1,0:T(8,128)(2,1)S(1)}, bf16[128,256]{1,0:T(8,128)(2,1)S(1)}, u32[]{:S(2)}, u32[]{:S(2)}) collective-permute-start(bf16[128,256]{1,0:T(8,128)(2,1)S(1)} %get-tuple-element.94), channel_id=1, source_target_pairs={{0,64},{16,80},{32,96},{48,112},{64,0},{80,16},{96,32},{112,48},{1... | collective-permute-start | bytes 196616 | tf_op jit(solution)/shard_map/ppermute | solution.py:22
  55.5 6.7 %collective-permute-start.18 = (bf16[2,128,256]{2,1,0:T(8,128)(2,1)S(1)}, bf16[2,128,256]{2,1,0:T(8,128)(2,1)S(1)}, u32[]{:S(2)}, u32[]{:S(2)}) collective-permute-start(bf16[2,128,256]{2,1,0:T(8,128)(2,1)S(1)} %get-tuple-element.99.refs_0_), channel_id=1, source_target_pairs={{0,3},{1,2},{2,1},{3,0},{4,7},{5,6},{6,5},{7,4},{8,11},{9,10},{10,... | collective-permute-start | bytes 393224 | tf_op jit(solution)/shard_map/ppermute | solution.py:22
  56.9 6.5 %collective-permute-start.17 = (bf16[2,128,256]{2,1,0:T(8,128)(2,1)S(1)}, bf16[2,128,256]{2,1,0:T(8,128)(2,1)S(1)}, u32[]{:S(2)}, u32[]{:S(2)}) collective-permute-start(bf16[2,128,256]{2,1,0:T(8,128)(2,1)S(1)} %get-tuple-element.99.refs_0_), channel_id=1, source_target_pairs={{0,2},{1,3},{2,0},{3,1},{4,6},{5,7},{6,4},{7,5},{8,10},{9,11},{10,... | collective-permute-start | bytes 393224 | tf_op jit(solution)/shard_map/ppermute | solution.py:22
  58.1 5.9 %collective-permute-start.16 = (bf16[2,128,256]{2,1,0:T(8,128)(2,1)S(1)}, bf16[2,128,256]{2,1,0:T(8,128)(2,1)S(1)}, u32[]{:S(2)}, u32[]{:S(2)}) collective-permute-start(bf16[2,128,256]{2,1,0:T(8,128)(2,1)S(1)} %get-tuple-element.99.refs_0_), channel_id=1, source_target_pairs={{0,1},{1,0},{2,3},{3,2},{4,5},{5,4},{6,7},{7,6},{8,9},{9,8},{10,11... | collective-permute-start | bytes 393224 | tf_op jit(solution)/shard_map/ppermute | solution.py:22
  69.3 5.5 %collective-permute-start.21 = (bf16[128,256]{1,0:T(8,128)(2,1)S(1)}, bf16[128,256]{1,0:T(8,128)(2,1)S(1)}, u32[]{:S(2)}, u32[]{:S(2)}) collective-permute-start(bf16[128,256]{1,0:T(8,128)(2,1)S(1)} %get-tuple-element.104), channel_id=1, source_target_pairs={{0,96},{16,112},{32,64},{48,80},{64,32},{80,48},{96,0},{112,16},{1... | collective-permute-start | bytes 196616 | tf_op jit(solution)/shard_map/ppermute | solution.py:22
  71.8 5.8 %collective-permute-start.22 = (bf16[128,256]{1,0:T(8,128)(2,1)S(1)}, bf16[128,256]{1,0:T(8,128)(2,1)S(1)}, u32[]{:S(2)}, u32[]{:S(2)}) collective-permute-start(bf16[128,256]{1,0:T(8,128)(2,1)S(1)} %get-tuple-element.105), channel_id=1, source_target_pairs={{0,64},{16,80},{32,96},{48,112},{64,0},{80,16},{96,32},{112,48},{1... | collective-permute-start | bytes 196616 | tf_op jit(solution)/shard_map/ppermute | solution.py:22
  83.0 6.7 %collective-permute-start.26 = (bf16[2,128,256]{2,1,0:T(8,128)(2,1)S(1)}, bf16[2,128,256]{2,1,0:T(8,128)(2,1)S(1)}, u32[]{:S(2)}, u32[]{:S(2)}) collective-permute-start(bf16[2,128,256]{2,1,0:T(8,128)(2,1)S(1)} %shard_map.111.refs_0_), channel_id=1, source_target_pairs={{0,3},{1,2},{2,1},{3,0},{4,7},{5,6},{6,5},{7,4},{8,11},{9,10},{10,... | collective-permute-start | bytes 393224 | tf_op jit(solution)/shard_map/ppermute | solution.py:22
  84.5 6.5 %collective-permute-start.25 = (bf16[2,128,256]{2,1,0:T(8,128)(2,1)S(1)}, bf16[2,128,256]{2,1,0:T(8,128)(2,1)S(1)}, u32[]{:S(2)}, u32[]{:S(2)}) collective-permute-start(bf16[2,128,256]{2,1,0:T(8,128)(2,1)S(1)} %shard_map.111.refs_0_), channel_id=1, source_target_pairs={{0,2},{1,3},{2,0},{3,1},{4,6},{5,7},{6,4},{7,5},{8,10},{9,11},{10,... | collective-permute-start | bytes 393224 | tf_op jit(solution)/shard_map/ppermute | solution.py:22
  85.8 5.8 %collective-permute-start.24 = (bf16[2,128,256]{2,1,0:T(8,128)(2,1)S(1)}, bf16[2,128,256]{2,1,0:T(8,128)(2,1)S(1)}, u32[]{:S(2)}, u32[]{:S(2)}) collective-permute-start(bf16[2,128,256]{2,1,0:T(8,128)(2,1)S(1)} %shard_map.111.refs_0_), channel_id=1, source_target_pairs={{0,1},{1,0},{2,3},{3,2},{4,5},{5,4},{6,7},{7,6},{8,9},{9,8},{10,11... | collective-permute-start | bytes 393224 | tf_op jit(solution)/shard_map/ppermute | solution.py:22
  96.3 8.3 %collective-permute-start.28 = (bf16[128,256]{1,0:T(8,128)(2,1)S(1)}, bf16[128,256]{1,0:T(8,128)(2,1)S(1)}, u32[]{:S(2)}, u32[]{:S(2)}) collective-permute-start(bf16[128,256]{1,0:T(8,128)(2,1)S(1)} %get-tuple-element.111), channel_id=1, source_target_pairs={{0,32},{16,48},{32,0},{48,16},{64,96},{80,112},{96,64},{112,80},{1... | collective-permute-start | bytes 196616 | tf_op jit(solution)/shard_map/ppermute | solution.py:22
  97.4 7.2 %collective-permute-start.29 = (bf16[128,256]{1,0:T(8,128)(2,1)S(1)}, bf16[128,256]{1,0:T(8,128)(2,1)S(1)}, u32[]{:S(2)}, u32[]{:S(2)}) collective-permute-start(bf16[128,256]{1,0:T(8,128)(2,1)S(1)} %get-tuple-element.112), channel_id=1, source_target_pairs={{0,96},{16,112},{32,64},{48,80},{64,32},{80,48},{96,0},{112,16},{1... | collective-permute-start | bytes 196616 | tf_op jit(solution)/shard_map/ppermute | solution.py:22
  98.1 6.5 %collective-permute-start.30 = (bf16[128,256]{1,0:T(8,128)(2,1)S(1)}, bf16[128,256]{1,0:T(8,128)(2,1)S(1)}, u32[]{:S(2)}, u32[]{:S(2)}) collective-permute-start(bf16[128,256]{1,0:T(8,128)(2,1)S(1)} %get-tuple-element.113), channel_id=1, source_target_pairs={{0,64},{16,80},{32,96},{48,112},{64,0},{80,16},{96,32},{112,48},{1... | collective-permute-start | bytes 196616 | tf_op jit(solution)/shard_map/ppermute | solution.py:22
  100.5 8.3 %collective-permute-start.35 = (bf16[144,256]{1,0:T(8,128)(2,1)S(1)}, bf16[144,256]{1,0:T(8,128)(2,1)S(1)}, u32[]{:S(2)}, u32[]{:S(2)}) collective-permute-start(bf16[144,256]{1,0:T(8,128)(2,1)S(1)} %get-tuple-element.117), channel_id=1, source_target_pairs={{0,8},{1,9},{2,10},{3,11},{4,12},{5,13},{6,14},{7,15},{8,0},{9,1},... | collective-permute-start | bytes 221192 | tf_op jit(solution)/shard_map/ppermute | solution.py:22
  103.5 6.1 %collective-permute-start.34 = (bf16[144,256]{1,0:T(8,128)(2,1)S(1)}, bf16[144,256]{1,0:T(8,128)(2,1)S(1)}, u32[]{:S(2)}, u32[]{:S(2)}) collective-permute-start(bf16[144,256]{1,0:T(8,128)(2,1)S(1)} %get-tuple-element.117), channel_id=1, source_target_pairs={{0,12},{1,13},{2,14},{3,15},{4,8},{5,9},{6,10},{7,11},{8,4},{9,5},... | collective-permute-start | bytes 221192 | tf_op jit(solution)/shard_map/ppermute | solution.py:22
  105.2 6.2 %collective-permute-start.33 = (bf16[128,256]{1,0:T(8,128)(2,1)S(1)}, bf16[128,256]{1,0:T(8,128)(2,1)S(1)}, u32[]{:S(2)}, u32[]{:S(2)}) collective-permute-start(bf16[128,256]{1,0:T(8,128)(2,1)S(1)} %get-tuple-element.116), channel_id=1, source_target_pairs={{0,8},{1,9},{2,10},{3,11},{4,12},{5,13},{6,14},{7,15},{8,0},{9,1},... | collective-permute-start | bytes 196616 | tf_op jit(solution)/shard_map/ppermute | solution.py:22
  107.6 5.5 %collective-permute-start.32 = (bf16[128,256]{1,0:T(8,128)(2,1)S(1)}, bf16[128,256]{1,0:T(8,128)(2,1)S(1)}, u32[]{:S(2)}, u32[]{:S(2)}) collective-permute-start(bf16[128,256]{1,0:T(8,128)(2,1)S(1)} %get-tuple-element.116), channel_id=1, source_target_pairs={{0,12},{1,13},{2,14},{3,15},{4,8},{5,9},{6,10},{7,11},{8,4},{9,5},... | collective-permute-start | bytes 196616 | tf_op jit(solution)/shard_map/ppermute | solution.py:22
  108.7 4.4 %collective-permute-start.31 = (bf16[128,256]{1,0:T(8,128)(2,1)S(1)}, bf16[128,256]{1,0:T(8,128)(2,1)S(1)}, u32[]{:S(2)}, u32[]{:S(2)}) collective-permute-start(bf16[128,256]{1,0:T(8,128)(2,1)S(1)} %get-tuple-element.116), channel_id=1, source_target_pairs={{0,4},{1,5},{2,6},{3,7},{4,0},{5,1},{6,2},{7,3},{8,12},{9,13},{10,... | collective-permute-start | bytes 196616 | tf_op jit(solution)/shard_map/ppermute | solution.py:22
  113.8 12.2 %collective-permute-start.38 = (bf16[4,128,256]{2,1,0:T(8,128)(2,1)S(1)}, bf16[4,128,256]{2,1,0:T(8,128)(2,1)S(1)}, u32[]{:S(2)}, u32[]{:S(2)}) collective-permute-start(bf16[4,128,256]{2,1,0:T(8,128)(2,1)S(1)} %shard_map.115.refs_0_), channel_id=1, source_target_pairs={{0,3},{1,2},{2,1},{3,0},{4,7},{5,6},{6,5},{7,4},{8,11},{9,10},{10,... | collective-permute-start | bytes 786440 | tf_op jit(solution)/shard_map/ppermute | solution.py:22
  115.2 10.7 %collective-permute-start.37 = (bf16[4,128,256]{2,1,0:T(8,128)(2,1)S(1)}, bf16[4,128,256]{2,1,0:T(8,128)(2,1)S(1)}, u32[]{:S(2)}, u32[]{:S(2)}) collective-permute-start(bf16[4,128,256]{2,1,0:T(8,128)(2,1)S(1)} %shard_map.115.refs_0_), channel_id=1, source_target_pairs={{0,2},{1,3},{2,0},{3,1},{4,6},{5,7},{6,4},{7,5},{8,10},{9,11},{10,... | collective-permute-start | bytes 786440 | tf_op jit(solution)/shard_map/ppermute | solution.py:22
  116.5 10.0 %collective-permute-start.36 = (bf16[4,128,256]{2,1,0:T(8,128)(2,1)S(1)}, bf16[4,128,256]{2,1,0:T(8,128)(2,1)S(1)}, u32[]{:S(2)}, u32[]{:S(2)}) collective-permute-start(bf16[4,128,256]{2,1,0:T(8,128)(2,1)S(1)} %shard_map.115.refs_0_), channel_id=1, source_target_pairs={{0,1},{1,0},{2,3},{3,2},{4,5},{5,4},{6,7},{7,6},{8,9},{9,8},{10,11... | collective-permute-start | bytes 786440 | tf_op jit(solution)/shard_map/ppermute | solution.py:22
  132.5 4.7 %collective-permute-start.40 = (bf16[128,256]{1,0:T(8,128)(2,1)S(1)}, bf16[128,256]{1,0:T(8,128)(2,1)S(1)}, u32[]{:S(2)}, u32[]{:S(2)}) collective-permute-start(bf16[128,256]{1,0:T(8,128)(2,1)S(1)} %get-tuple-element.121), channel_id=1, source_target_pairs={{0,32},{16,48},{32,0},{48,16},{64,96},{80,112},{96,64},{112,80},{1... | collective-permute-start | bytes 196616 | tf_op jit(solution)/shard_map/ppermute | solution.py:22
  133.6 5.5 %collective-permute-start.41 = (bf16[128,256]{1,0:T(8,128)(2,1)S(1)}, bf16[128,256]{1,0:T(8,128)(2,1)S(1)}, u32[]{:S(2)}, u32[]{:S(2)}) collective-permute-start(bf16[128,256]{1,0:T(8,128)(2,1)S(1)} %get-tuple-element.122), channel_id=1, source_target_pairs={{0,96},{16,112},{32,64},{48,80},{64,32},{80,48},{96,0},{112,16},{1... | collective-permute-start | bytes 196616 | tf_op jit(solution)/shard_map/ppermute | solution.py:22
  136.2 5.8 %collective-permute-start.42 = (bf16[128,256]{1,0:T(8,128)(2,1)S(1)}, bf16[128,256]{1,0:T(8,128)(2,1)S(1)}, u32[]{:S(2)}, u32[]{:S(2)}) collective-permute-start(bf16[128,256]{1,0:T(8,128)(2,1)S(1)} %get-tuple-element.123), channel_id=1, source_target_pairs={{0,64},{16,80},{32,96},{48,112},{64,0},{80,16},{96,32},{112,48},{1... | collective-permute-start | bytes 196616 | tf_op jit(solution)/shard_map/ppermute | solution.py:22
  142.6 6.1 %collective-permute-start.45 = (bf16[256,128]{1,0:T(8,128)(2,1)S(1)}, bf16[256,128]{1,0:T(8,128)(2,1)S(1)}, u32[]{:S(2)}, u32[]{:S(2)}) collective-permute-start(bf16[256,128]{1,0:T(8,128)(2,1)S(1)} %shard_map.118.refs_0_), channel_id=1, source_target_pairs={{0,64},{16,80},{32,96},{48,112},{64,0},{80,16},{96,32},{112,48},{1... | collective-permute-start | bytes 196616 | tf_op jit(solution)/shard_map/ppermute | solution.py:22
  143.7 5.6 %collective-permute-start.44 = (bf16[256,128]{1,0:T(8,128)(2,1)S(1)}, bf16[256,128]{1,0:T(8,128)(2,1)S(1)}, u32[]{:S(2)}, u32[]{:S(2)}) collective-permute-start(bf16[256,128]{1,0:T(8,128)(2,1)S(1)} %shard_map.118.refs_0_), channel_id=1, source_target_pairs={{0,96},{16,112},{32,64},{48,80},{64,32},{80,48},{96,0},{112,16},{1... | collective-permute-start | bytes 196616 | tf_op jit(solution)/shard_map/ppermute | solution.py:22
  156.2 9.2 %collective-permute-start.50 = (bf16[4,256,128]{2,1,0:T(8,128)(2,1)S(1)}, bf16[4,256,128]{2,1,0:T(8,128)(2,1)S(1)}, u32[]{:S(2)}, u32[]{:S(2)}) collective-permute-start(bf16[4,256,128]{2,1,0:T(8,128)(2,1)S(1)} %get-tuple-element.125), channel_id=1, source_target_pairs={{0,1},{1,0},{2,3},{3,2},{4,5},{5,4},{6,7},{7,6},{8,9},{9,8},{10,11... | collective-permute-start | bytes 786440 | tf_op jit(solution)/shard_map/ppermute | solution.py:22
  156.9 14.9 %collective-permute-start.51 = (bf16[4,256,128]{2,1,0:T(8,128)(2,1)S(1)}, bf16[4,256,128]{2,1,0:T(8,128)(2,1)S(1)}, u32[]{:S(2)}, u32[]{:S(2)}) collective-permute-start(bf16[4,256,128]{2,1,0:T(8,128)(2,1)S(1)} %get-tuple-element.126), channel_id=1, source_target_pairs={{0,3},{1,2},{2,1},{3,0},{4,7},{5,6},{6,5},{7,4},{8,11},{9,10},{10,... | collective-permute-start | bytes 786440 | tf_op jit(solution)/shard_map/ppermute | solution.py:22
  158.9 13.0 %collective-permute-start.52 = (bf16[4,256,128]{2,1,0:T(8,128)(2,1)S(1)}, bf16[4,256,128]{2,1,0:T(8,128)(2,1)S(1)}, u32[]{:S(2)}, u32[]{:S(2)}) collective-permute-start(bf16[4,256,128]{2,1,0:T(8,128)(2,1)S(1)} %get-tuple-element.127), channel_id=1, source_target_pairs={{0,2},{1,3},{2,0},{3,1},{4,6},{5,7},{6,4},{7,5},{8,10},{9,11},{10,... | collective-permute-start | bytes 786440 | tf_op jit(solution)/shard_map/ppermute | solution.py:22
  172.5 6.0 %collective-permute-start.53 = (bf16[2,256,128]{2,1,0:T(8,128)(2,1)S(1)}, bf16[2,256,128]{2,1,0:T(8,128)(2,1)S(1)}, u32[]{:S(2)}, u32[]{:S(2)}) collective-permute-start(bf16[2,256,128]{2,1,0:T(8,128)(2,1)S(1)} %get-tuple-element.129), channel_id=1, source_target_pairs={{0,4},{1,5},{2,6},{3,7},{4,0},{5,1},{6,2},{7,3},{8,12},{9,13},{10,... | collective-permute-start | bytes 393224 | tf_op jit(solution)/shard_map/ppermute | solution.py:22
  172.6 8.3 %collective-permute-start.54 = (bf16[2,256,128]{2,1,0:T(8,128)(2,1)S(1)}, bf16[2,256,128]{2,1,0:T(8,128)(2,1)S(1)}, u32[]{:S(2)}, u32[]{:S(2)}) collective-permute-start(bf16[2,256,128]{2,1,0:T(8,128)(2,1)S(1)} %get-tuple-element.130), channel_id=1, source_target_pairs={{0,12},{1,13},{2,14},{3,15},{4,8},{5,9},{6,10},{7,11},{8,4},{9,5},... | collective-permute-start | bytes 393224 | tf_op jit(solution)/shard_map/ppermute | solution.py:22
  174.1 6.8 %collective-permute-start.55 = (bf16[2,256,128]{2,1,0:T(8,128)(2,1)S(1)}, bf16[2,256,128]{2,1,0:T(8,128)(2,1)S(1)}, u32[]{:S(2)}, u32[]{:S(2)}) collective-permute-start(bf16[2,256,128]{2,1,0:T(8,128)(2,1)S(1)} %get-tuple-element.131), channel_id=1, source_target_pairs={{0,8},{1,9},{2,10},{3,11},{4,12},{5,13},{6,14},{7,15},{8,0},{9,1},... | collective-permute-start | bytes 393224 | tf_op jit(solution)/shard_map/ppermute | solution.py:22
  181.5 5.8 %collective-permute-start.58 = (bf16[256,128]{1,0:T(8,128)(2,1)S(1)}, bf16[256,128]{1,0:T(8,128)(2,1)S(1)}, u32[]{:S(2)}, u32[]{:S(2)}) collective-permute-start(bf16[256,128]{1,0:T(8,128)(2,1)S(1)} %get-tuple-element.132.refs_0_.down_ref), channel_id=1, source_target_pairs={{0,64},{16,80},{32,96},{48,112},{64,0},{80,16},{96,32},{112,48},{1... | collective-permute-start | bytes 196616 | tf_op jit(solution)/shard_map/ppermute | solution.py:22
  182.7 5.5 %collective-permute-start.57 = (bf16[256,128]{1,0:T(8,128)(2,1)S(1)}, bf16[256,128]{1,0:T(8,128)(2,1)S(1)}, u32[]{:S(2)}, u32[]{:S(2)}) collective-permute-start(bf16[256,128]{1,0:T(8,128)(2,1)S(1)} %get-tuple-element.132.refs_0_.down_ref), channel_id=1, source_target_pairs={{0,96},{16,112},{32,64},{48,80},{64,32},{80,48},{96,0},{112,16},{1... | collective-permute-start | bytes 196616 | tf_op jit(solution)/shard_map/ppermute | solution.py:22
  192.4 6.3 %collective-permute-start.63 = (bf16[2,256,128]{2,1,0:T(8,128)(2,1)S(1)}, bf16[2,256,128]{2,1,0:T(8,128)(2,1)S(1)}, u32[]{:S(2)}, u32[]{:S(2)}) collective-permute-start(bf16[2,256,128]{2,1,0:T(8,128)(2,1)S(1)} %get-tuple-element.134), channel_id=1, source_target_pairs={{0,1},{1,0},{2,3},{3,2},{4,5},{5,4},{6,7},{7,6},{8,9},{9,8},{10,11... | collective-permute-start | bytes 393224 | tf_op jit(solution)/shard_map/ppermute | solution.py:22
  193.0 9.4 %collective-permute-start.64 = (bf16[2,256,128]{2,1,0:T(8,128)(2,1)S(1)}, bf16[2,256,128]{2,1,0:T(8,128)(2,1)S(1)}, u32[]{:S(2)}, u32[]{:S(2)}) collective-permute-start(bf16[2,256,128]{2,1,0:T(8,128)(2,1)S(1)} %get-tuple-element.135), channel_id=1, source_target_pairs={{0,3},{1,2},{2,1},{3,0},{4,7},{5,6},{6,5},{7,4},{8,11},{9,10},{10,... | collective-permute-start | bytes 393224 | tf_op jit(solution)/shard_map/ppermute | solution.py:22
  194.6 7.7 %collective-permute-start.65 = (bf16[2,256,128]{2,1,0:T(8,128)(2,1)S(1)}, bf16[2,256,128]{2,1,0:T(8,128)(2,1)S(1)}, u32[]{:S(2)}, u32[]{:S(2)}) collective-permute-start(bf16[2,256,128]{2,1,0:T(8,128)(2,1)S(1)} %get-tuple-element.136), channel_id=1, source_target_pairs={{0,2},{1,3},{2,0},{3,1},{4,6},{5,7},{6,4},{7,5},{8,10},{9,11},{10,... | collective-permute-start | bytes 393224 | tf_op jit(solution)/shard_map/ppermute | solution.py:22
  207.9 6.3 %collective-permute-start.69 = (bf16[256,128]{1,0:T(8,128)(2,1)S(1)}, bf16[256,128]{1,0:T(8,128)(2,1)S(1)}, u32[]{:S(2)}, u32[]{:S(2)}) collective-permute-start(bf16[256,128]{1,0:T(8,128)(2,1)S(1)} %shard_map.124.refs_0_), channel_id=1, source_target_pairs={{0,64},{16,80},{32,96},{48,112},{64,0},{80,16},{96,32},{112,48},{1... | collective-permute-start | bytes 196616 | tf_op jit(solution)/shard_map/ppermute | solution.py:22
  210.0 5.5 %collective-permute-start.68 = (bf16[256,128]{1,0:T(8,128)(2,1)S(1)}, bf16[256,128]{1,0:T(8,128)(2,1)S(1)}, u32[]{:S(2)}, u32[]{:S(2)}) collective-permute-start(bf16[256,128]{1,0:T(8,128)(2,1)S(1)} %shard_map.124.refs_0_), channel_id=1, source_target_pairs={{0,96},{16,112},{32,64},{48,80},{64,32},{80,48},{96,0},{112,16},{1... | collective-permute-start | bytes 196616 | tf_op jit(solution)/shard_map/ppermute | solution.py:22
  211.5 4.5 %collective-permute-start.70 = (bf16[256,128]{1,0:T(8,128)(2,1)S(1)}, bf16[256,128]{1,0:T(8,128)(2,1)S(1)}, u32[]{:S(2)}, u32[]{:S(2)}) collective-permute-start(bf16[256,128]{1,0:T(8,128)(2,1)S(1)} %shard_map.124.refs_0_), channel_id=1, source_target_pairs={{0,16},{16,0},{32,48},{48,32},{64,80},{80,64},{96,112},{112,96},{1... | collective-permute-start | bytes 196616 | tf_op jit(solution)/shard_map/ppermute | solution.py:22
  219.6 6.4 %collective-permute-start.74 = (bf16[2,256,128]{2,1,0:T(8,128)(2,1)S(1)}, bf16[2,256,128]{2,1,0:T(8,128)(2,1)S(1)}, u32[]{:S(2)}, u32[]{:S(2)}) collective-permute-start(bf16[2,256,128]{2,1,0:T(8,128)(2,1)S(1)} %get-tuple-element.140), channel_id=1, source_target_pairs={{0,1},{1,0},{2,3},{3,2},{4,5},{5,4},{6,7},{7,6},{8,9},{9,8},{10,11... | collective-permute-start | bytes 393224 | tf_op jit(solution)/shard_map/ppermute | solution.py:22
  219.9 7.7 %collective-permute-start.75 = (bf16[2,256,128]{2,1,0:T(8,128)(2,1)S(1)}, bf16[2,256,128]{2,1,0:T(8,128)(2,1)S(1)}, u32[]{:S(2)}, u32[]{:S(2)}) collective-permute-start(bf16[2,256,128]{2,1,0:T(8,128)(2,1)S(1)} %get-tuple-element.141), channel_id=1, source_target_pairs={{0,3},{1,2},{2,1},{3,0},{4,7},{5,6},{6,5},{7,4},{8,11},{9,10},{10,... | collective-permute-start | bytes 393224 | tf_op jit(solution)/shard_map/ppermute | solution.py:22
  221.7 7.7 %collective-permute-start.76 = (bf16[2,256,128]{2,1,0:T(8,128)(2,1)S(1)}, bf16[2,256,128]{2,1,0:T(8,128)(2,1)S(1)}, u32[]{:S(2)}, u32[]{:S(2)}) collective-permute-start(bf16[2,256,128]{2,1,0:T(8,128)(2,1)S(1)} %get-tuple-element.142), channel_id=1, source_target_pairs={{0,2},{1,3},{2,0},{3,1},{4,6},{5,7},{6,4},{7,5},{8,10},{9,11},{10,... | collective-permute-start | bytes 393224 | tf_op jit(solution)/shard_map/ppermute | solution.py:22
  230.0 6.3 %collective-permute-start.77 = (bf16[3,256,128]{2,1,0:T(8,128)(2,1)S(1)}, bf16[3,256,128]{2,1,0:T(8,128)(2,1)S(1)}, u32[]{:S(2)}, u32[]{:S(2)}) collective-permute-start(bf16[3,256,128]{2,1,0:T(8,128)(2,1)S(1)} %get-tuple-element.144), channel_id=1, source_target_pairs={{0,4},{1,5},{2,6},{3,7},{4,0},{5,1},{6,2},{7,3},{8,12},{9,13},{10,... | collective-permute-start | bytes 589832 | tf_op jit(solution)/shard_map/ppermute | solution.py:22
  236.9 5.8 %collective-permute-start.80 = (bf16[256,128]{1,0:T(8,128)(2,1)S(1)}, bf16[256,128]{1,0:T(8,128)(2,1)S(1)}, u32[]{:S(2)}, u32[]{:S(2)}) collective-permute-start(bf16[256,128]{1,0:T(8,128)(2,1)S(1)} %get-tuple-element.146.refs_0_.refs_8_), channel_id=1, source_target_pairs={{0,64},{16,80},{32,96},{48,112},{64,0},{80,16},{96,32},{112,48},{1... | collective-permute-start | bytes 196616 | tf_op jit(solution)/shard_map/ppermute | solution.py:22
  238.0 5.5 %collective-permute-start.79 = (bf16[256,128]{1,0:T(8,128)(2,1)S(1)}, bf16[256,128]{1,0:T(8,128)(2,1)S(1)}, u32[]{:S(2)}, u32[]{:S(2)}) collective-permute-start(bf16[256,128]{1,0:T(8,128)(2,1)S(1)} %get-tuple-element.146.refs_0_.refs_8_), channel_id=1, source_target_pairs={{0,96},{16,112},{32,64},{48,80},{64,32},{80,48},{96,0},{112,16},{1... | collective-permute-start | bytes 196616 | tf_op jit(solution)/shard_map/ppermute | solution.py:22
  246.6 5.6 %collective-permute-start.86 = (bf16[1,256,128]{2,1,0:T(8,128)(2,1)S(1)}, bf16[1,256,128]{2,1,0:T(8,128)(2,1)S(1)}, u32[]{:S(2)}, u32[]{:S(2)}) collective-permute-start(bf16[1,256,128]{2,1,0:T(8,128)(2,1)S(1)} %get-tuple-element.149), channel_id=1, source_target_pairs={{0,3},{1,2},{2,1},{3,0},{4,7},{5,6},{6,5},{7,4},{8,11},{9,10},{10,... | collective-permute-start | bytes 196616 | tf_op jit(solution)/shard_map/ppermute | solution.py:22
  248.5 5.8 %collective-permute-start.87 = (bf16[1,256,128]{2,1,0:T(8,128)(2,1)S(1)}, bf16[1,256,128]{2,1,0:T(8,128)(2,1)S(1)}, u32[]{:S(2)}, u32[]{:S(2)}) collective-permute-start(bf16[1,256,128]{2,1,0:T(8,128)(2,1)S(1)} %get-tuple-element.150), channel_id=1, source_target_pairs={{0,2},{1,3},{2,0},{3,1},{4,6},{5,7},{6,4},{7,5},{8,10},{9,11},{10,... | collective-permute-start | bytes 196616 | tf_op jit(solution)/shard_map/ppermute | solution.py:22
  254.9 6.6 %collective-permute-start.90 = (bf16[256,128]{1,0:T(8,128)(2,1)S(1)}, bf16[256,128]{1,0:T(8,128)(2,1)S(1)}, u32[]{:S(2)}, u32[]{:S(2)}) collective-permute-start(bf16[256,128]{1,0:T(8,128)(2,1)S(1)} %shard_map.129.refs_0_), channel_id=1, source_target_pairs={{0,64},{16,80},{32,96},{48,112},{64,0},{80,16},{96,32},{112,48},{1... | collective-permute-start | bytes 196616 | tf_op jit(solution)/shard_map/ppermute | solution.py:22
  256.9 5.5 %collective-permute-start.89 = (bf16[256,128]{1,0:T(8,128)(2,1)S(1)}, bf16[256,128]{1,0:T(8,128)(2,1)S(1)}, u32[]{:S(2)}, u32[]{:S(2)}) collective-permute-start(bf16[256,128]{1,0:T(8,128)(2,1)S(1)} %shard_map.129.refs_0_), channel_id=1, source_target_pairs={{0,96},{16,112},{32,64},{48,80},{64,32},{80,48},{96,0},{112,16},{1... | collective-permute-start | bytes 196616 | tf_op jit(solution)/shard_map/ppermute | solution.py:22
  258.5 4.4 %collective-permute-start.91 = (bf16[256,128]{1,0:T(8,128)(2,1)S(1)}, bf16[256,128]{1,0:T(8,128)(2,1)S(1)}, u32[]{:S(2)}, u32[]{:S(2)}) collective-permute-start(bf16[256,128]{1,0:T(8,128)(2,1)S(1)} %shard_map.129.refs_0_), channel_id=1, source_target_pairs={{0,16},{16,0},{32,48},{48,32},{64,80},{80,64},{96,112},{112,96},{1... | collective-permute-start | bytes 196616 | tf_op jit(solution)/shard_map/ppermute | solution.py:22
  265.4 11.4 %collective-permute-start.97 = (bf16[3,256,128]{2,1,0:T(8,128)(2,1)S(1)}, bf16[3,256,128]{2,1,0:T(8,128)(2,1)S(1)}, u32[]{:S(2)}, u32[]{:S(2)}) collective-permute-start(bf16[3,256,128]{2,1,0:T(8,128)(2,1)S(1)} %get-tuple-element.154), channel_id=1, source_target_pairs={{0,2},{1,3},{2,0},{3,1},{4,6},{5,7},{6,4},{7,5},{8,10},{9,11},{10,... | collective-permute-start | bytes 589832 | tf_op jit(solution)/shard_map/ppermute | solution.py:22
  267.8 7.9 %collective-permute-start.95 = (bf16[2,256,128]{2,1,0:T(8,128)(2,1)S(1)}, bf16[2,256,128]{2,1,0:T(8,128)(2,1)S(1)}, u32[]{:S(2)}, u32[]{:S(2)}) collective-permute-start(bf16[2,256,128]{2,1,0:T(8,128)(2,1)S(1)} %get-tuple-element.152), channel_id=1, source_target_pairs={{0,1},{1,0},{2,3},{3,2},{4,5},{5,4},{6,7},{7,6},{8,9},{9,8},{10,11... | collective-permute-start | bytes 393224 | tf_op jit(solution)/shard_map/ppermute | solution.py:22
  267.9 8.8 %collective-permute-start.96 = (bf16[2,256,128]{2,1,0:T(8,128)(2,1)S(1)}, bf16[2,256,128]{2,1,0:T(8,128)(2,1)S(1)}, u32[]{:S(2)}, u32[]{:S(2)}) collective-permute-start(bf16[2,256,128]{2,1,0:T(8,128)(2,1)S(1)} %get-tuple-element.153), channel_id=1, source_target_pairs={{0,3},{1,2},{2,1},{3,0},{4,7},{5,6},{6,5},{7,4},{8,11},{9,10},{10,... | collective-permute-start | bytes 393224 | tf_op jit(solution)/shard_map/ppermute | solution.py:22
  (43 other events, 248.0 us)
